TPU v7x, 128 devices: a whole 4x4x4 slice. The times are simulated.
128 devices in a mesh: dp: 64 (over y, x, z_lo, core), tensor: 2 (over z_hi).
Axes of the slice: x: 4, y: 4, z: 4 (z_hi: 2, z_lo: 2; z = z_hi * 2 + z_lo), core: 2. Of those that a mesh axis runs over, the one named last changes fastest.
Arguments:
- tokens: bfloat16 [16384, 1152], P('dp'), may hold values from -6 to 6
- cotangent: bfloat16 [16384, 1152], P('dp'), may hold values from -16 to 16
- input_gain: bfloat16 [1152], P('dp'), may hold values from 0.25 to 1.75
- query_weight: bfloat16 [1152, 1024], P('dp', 'tensor'), may hold values from -0.1875 to 0.1875
- key_weight: bfloat16 [1152, 256], P('dp'), may hold values from -0.1875 to 0.1875
- value_weight: bfloat16 [1152, 256], P('dp'), may hold values from -0.1875 to 0.1875
- query_gain: bfloat16 [256], P('dp'), may hold values from 0.25 to 1.75
- key_gain: bfloat16 [256], P('dp'), may hold values from 0.25 to 1.75
- output_weight: bfloat16 [1024, 1152], P('tensor', 'dp'), may hold values from -0.1875 to 0.1875
- attention_gain: bfloat16 [1152], P('dp'), may hold values from 0.25 to 1.75
- feed_gain: bfloat16 [1152], P('dp'), may hold values from 0.25 to 1.75
- gate_weight: bfloat16 [1152, 6912], P('dp', 'tensor'), may hold values from -0.1875 to 0.1875
- up_weight: bfloat16 [1152, 6912], P('dp', 'tensor'), may hold values from -0.1875 to 0.1875
- down_weight: bfloat16 [6912, 1152], P('tensor', 'dp'), may hold values from -0.078125 to 0.078125
- output_gain: bfloat16 [1152], P('dp'), may hold values from 0.25 to 1.75
Outputs:
- layer_out: bfloat16 [16384, 1152], P('dp')
- input_grad: float32 [16384, 1152], P('dp')
- input_gain_grad: float32 [1152], P('dp')
- query_weight_grad: float32 [1152, 1024], P('dp', 'tensor')
- key_weight_grad: float32 [1152, 256], P('dp')
- value_weight_grad: float32 [1152, 256], P('dp')
- query_gain_grad: float32 [256], P('dp')
- key_gain_grad: float32 [256], P('dp')
- output_weight_grad: float32 [1024, 1152], P('tensor', 'dp')
- attention_gain_grad: float32 [1152], P('dp')
- feed_gain_grad: float32 [1152], P('dp')
- gate_weight_grad: float32 [1152, 6912], P('dp', 'tensor')
- up_weight_grad: float32 [1152, 6912], P('dp', 'tensor')
- down_weight_grad: float32 [6912, 1152], P('tensor', 'dp')
- output_gain_grad: float32 [1152], P('dp')
All inputs are finite; a program needn't handle non-finite values.
Results may differ from a plain program's by a relative error of at most 0.024.
Values may be sent and summed in bfloat16 or wider, within the bound.
No kernel may reach another device: no remote copies, remote signals or barrier semaphores. Data moves between devices by JAX's collectives and lax.ppermute only.
A program may use at most 320 MiB of HBM per device.

v0:
```python
import jax
import jax.numpy as jnp
from jax import lax
from jax.sharding import PartitionSpec as P

HD = 256


EPS = 1e-06
THETA = 1000000.0


def sent_together(arrays, axis, dim, along):
    columns = [a.reshape(*a.shape[:along], -1) for a in arrays]
    both = jnp.concatenate(columns, axis=along)
    out, at, outs = (lax.all_gather(both, axis, axis=dim, tiled=True), 0, [])
    for a, column in zip(arrays, columns):
        section = out[..., at : at + column.shape[along]]
        outs.append(section.reshape(*section.shape[:along], *a.shape[along:]))
        at += column.shape[along]
    return tuple(outs)


def rows_first(arrays, axis, dims):
    turned = [jnp.moveaxis(a, dim, 0) for a, dim in zip(arrays, dims)]
    both = jnp.concatenate([t.reshape(len(t), -1) for t in turned], axis=1)
    out, at, outs = (lax.all_gather(both, axis, axis=0, tiled=True), 0, [])
    for t, dim in zip(turned, dims):
        section = out[:, at : at + t[0].size].reshape(-1, *t.shape[1:])
        outs.append(jnp.moveaxis(section, 0, dim))
        at += t[0].size
    return tuple(outs)


def from_everyone(shard, axis):
    copies = jnp.broadcast_to(shard, (lax.axis_size(axis), *shard.shape))
    return lax.all_to_all(copies, axis, split_axis=0, concat_axis=0, tiled=True)


def taken_together(shard, axis):
    everything = from_everyone(shard, axis)
    return jnp.sum(everything, axis=0)


def taken_together_2(shard, axis):
    return from_everyone(shard, axis).astype(jnp.float32).sum(axis=0)


def normalize(field, gain):
    return field * lax.rsqrt(jnp.mean(field * field, axis=-1, keepdims=True) + EPS) * gain


def rotate(field):
    length = field.shape[-3]
    half = field.shape[-1] // 2
    freq = THETA ** (-jnp.arange(half, dtype=jnp.float32) / half)
    angle = jnp.arange(length, dtype=jnp.float32)[:, None] * freq[None, :]
    cosine = jnp.cos(angle)[:, None, :]
    sine = jnp.sin(angle)[:, None, :]
    first = field[..., :half]
    second = field[..., half:]
    return jnp.concatenate(
        [first * cosine - second * sine, second * cosine + first * sine], axis=-1
    )


def prepare(field, gain):
    return rotate(normalize(field, gain))


def activate(gate, upper):
    return jax.nn.gelu(gate, approximate=True) * upper


def product(left, right):
    return jnp.dot(left, right, preferred_element_type=jnp.float32)


def contract_rows(left, right):
    return lax.dot_general(
        left, right, (((0,), (0,)), ((), ())), preferred_element_type=jnp.float32
    )


def contract_cols(left, right):
    return lax.dot_general(
        left, right, (((1,), (1,)), ((), ())), preferred_element_type=jnp.float32
    )


def causal_scores(query_block, keys_low, start, scale):
    scores = (
        jnp.einsum("qhd,kd->hqk", query_block, keys_low, preferred_element_type=jnp.float32) * scale
    )
    rows = start + jnp.arange(query_block.shape[0])[:, None]
    cols = jnp.arange(keys_low.shape[0])[None, :]
    return jnp.where(cols <= rows, scores, -1e30)


def on_device(
    tokens,
    cotangent,
    input_gain,
    query_weight,
    key_weight,
    value_weight,
    query_gain,
    key_gain,
    output_weight,
    attention_gain,
    feed_gain,
    gate_weight,
    up_weight,
    down_weight,
    output_gain,
):
    (
        norm_gain,
        query_matrix,
        key_matrix,
        value_matrix,
        query_scale,
        key_scale,
        output_matrix,
        post_gain,
    ) = (
        *sent_together((input_gain, query_weight, key_weight, value_weight), "dp", 0, 1),
        lax.all_gather(query_gain, "dp", axis=0, tiled=True),
        lax.all_gather(key_gain, "dp", axis=0, tiled=True),
        lax.all_gather(output_weight, "dp", axis=1, tiled=True),
        lax.all_gather(attention_gain, "dp", axis=0, tiled=True),
    )
    feed_scale, gate_matrix, up_matrix, down_matrix, final_gain = rows_first(
        (feed_gain, gate_weight, up_weight, down_weight, output_gain), "dp", (0, 0, 0, 1, 0)
    )
    norm_gain = norm_gain.astype(jnp.float32)
    query_scale = query_scale.astype(jnp.float32)
    key_scale = key_scale.astype(jnp.float32)
    post_gain = post_gain.astype(jnp.float32)
    feed_scale = feed_scale.astype(jnp.float32)
    final_gain = final_gain.astype(jnp.float32)
    rows = tokens.astype(jnp.float32)
    length = rows.shape[0]
    heads = query_matrix.shape[1] // HD
    scale = HD ** (-0.5)
    width = min(512, length)
    count = length // width
    normed_full, input_pull = jax.vjp(normalize, rows, norm_gain)
    normed = normed_full.astype(jnp.bfloat16)
    queries = product(normed, query_matrix).reshape(length, heads, HD)
    keys = product(normed, key_matrix).reshape(length, 1, HD)
    values_low = product(normed, value_matrix).astype(jnp.bfloat16)
    queries_rot, query_pull = jax.vjp(prepare, queries, query_scale)
    keys_rot, key_pull = jax.vjp(prepare, keys, key_scale)
    queries_low = queries_rot.astype(jnp.bfloat16)
    keys_low = keys_rot[:, 0, :].astype(jnp.bfloat16)
    query_blocks = queries_low.reshape(count, width, heads, HD)
    block_index = jnp.arange(count)

    def forward_block(pair):
        block, index = pair
        scores = causal_scores(block, keys_low, index * width, scale)
        peak = jnp.max(scores, axis=-1, keepdims=True)
        expo = jnp.exp(scores - peak)
        total = jnp.sum(expo, axis=-1, keepdims=True)
        weights = (expo / total).astype(jnp.bfloat16)
        mixed_block = jnp.einsum(
            "hqk,kd->qhd", weights, values_low, preferred_element_type=jnp.float32
        )
        return (mixed_block.astype(jnp.bfloat16), peak[..., 0] + jnp.log(total[..., 0]))

    mixed, log_totals = lax.map(forward_block, (query_blocks, block_index))
    mixed = mixed.reshape(length, heads * HD)
    branch = taken_together(product(mixed, output_matrix), "tensor")
    post_value, post_pull = jax.vjp(normalize, branch, post_gain)
    hidden_state = rows + post_value
    feed_full, feed_pull = jax.vjp(normalize, hidden_state, feed_scale)
    feed_low = feed_full.astype(jnp.bfloat16)
    gate = product(feed_low, gate_matrix)
    upper = product(feed_low, up_matrix)
    activ_full, act_pull = jax.vjp(activate, gate, upper)
    activ = activ_full.astype(jnp.bfloat16)
    second = taken_together_2(product(activ, down_matrix).astype(jnp.bfloat16), "tensor").astype(
        jnp.float32
    )
    final_value, final_pull = jax.vjp(normalize, second, final_gain)
    layer_out = (hidden_state + final_value).astype(jnp.bfloat16)
    upstream = cotangent.astype(jnp.float32)
    grad_second, grad_final_gain = final_pull(upstream)
    grad_second = grad_second.astype(jnp.bfloat16)
    grad_down = contract_rows(activ, grad_second)
    grad_activ = contract_cols(grad_second, down_matrix)
    grad_gate, grad_upper = act_pull(grad_activ)
    grad_gate = grad_gate.astype(jnp.bfloat16)
    grad_upper = grad_upper.astype(jnp.bfloat16)
    feed_back = taken_together_2(
        (contract_cols(grad_gate, gate_matrix) + contract_cols(grad_upper, up_matrix)).astype(
            jnp.bfloat16
        ),
        "tensor",
    ).astype(jnp.float32)
    grad_hidden_add, grad_feed_gain = feed_pull(feed_back)
    grad_hidden = upstream + grad_hidden_add
    grad_gate_weight = contract_rows(feed_low, grad_gate)
    grad_up_weight = contract_rows(feed_low, grad_upper)
    grad_branch, grad_post_gain = post_pull(grad_hidden)
    grad_branch = grad_branch.astype(jnp.bfloat16)
    grad_output_weight = contract_rows(mixed, grad_branch)
    grad_mixed = contract_cols(grad_branch, output_matrix).astype(jnp.bfloat16)
    grad_blocks = grad_mixed.reshape(count, width, heads, HD)

    def backward_block(carry, quad):
        key_total, value_total = carry
        block, grad_block, lse_block, index = quad
        scores = causal_scores(block, keys_low, index * width, scale)
        weights = jnp.exp(scores - lse_block[..., None])
        grad_weights = jnp.einsum(
            "qhd,kd->hqk", grad_block, values_low, preferred_element_type=jnp.float32
        )
        center = jnp.sum(weights * grad_weights, axis=-1, keepdims=True)
        grad_scores = (weights * (grad_weights - center)).astype(jnp.bfloat16)
        query_grad = (
            jnp.einsum("hqk,kd->qhd", grad_scores, keys_low, preferred_element_type=jnp.float32)
            * scale
        )
        key_total = (
            key_total
            + jnp.einsum("hqk,qhd->kd", grad_scores, block, preferred_element_type=jnp.float32)
            * scale
        )
        value_total = value_total + jnp.einsum(
            "hqk,qhd->kd",
            weights.astype(jnp.bfloat16),
            grad_block,
            preferred_element_type=jnp.float32,
        )
        return ((key_total, value_total), query_grad)

    empty = jnp.zeros((length, HD), jnp.float32)
    (grad_keys_rot, grad_values), grad_queries_rot = lax.scan(
        backward_block, (empty, empty), (query_blocks, grad_blocks, log_totals, block_index)
    )
    grad_queries, grad_query_scale = query_pull(grad_queries_rot.reshape(length, heads, HD))
    grad_queries = grad_queries.reshape(length, heads * HD).astype(jnp.bfloat16)
    grad_query_weight = contract_rows(normed, grad_queries)
    query_back, keys_summed, values_summed, query_scale_grad = (
        taken_together_2(
            contract_cols(grad_queries, query_matrix).astype(jnp.bfloat16), "tensor"
        ).astype(jnp.float32),
        taken_together_2(grad_keys_rot.astype(jnp.bfloat16), "tensor").astype(jnp.float32),
        taken_together_2(grad_values.astype(jnp.bfloat16), "tensor").astype(jnp.float32),
        taken_together_2(grad_query_scale.astype(jnp.bfloat16), "tensor").astype(jnp.float32),
    )
    grad_keys, grad_key_scale = key_pull(keys_summed.reshape(length, 1, HD))
    grad_keys = grad_keys.reshape(length, HD).astype(jnp.bfloat16)
    grad_values_low = values_summed.astype(jnp.bfloat16)
    grad_key_weight = contract_rows(normed, grad_keys)
    grad_value_weight = contract_rows(normed, grad_values_low)
    grad_normed = (
        query_back
        + contract_cols(grad_keys, key_matrix)
        + contract_cols(grad_values_low, value_matrix)
    )
    grad_rows_add, grad_norm_gain = input_pull(grad_normed)
    input_grad = grad_hidden + grad_rows_add
    summed_all = (
        lax.psum_scatter(grad_norm_gain, "dp", scatter_dimension=0, tiled=True),
        lax.psum_scatter(grad_query_weight, "dp", scatter_dimension=0, tiled=True),
        lax.psum_scatter(grad_key_weight, "dp", scatter_dimension=0, tiled=True),
        lax.psum_scatter(grad_value_weight, "dp", scatter_dimension=0, tiled=True),
        lax.psum_scatter(query_scale_grad, "dp", scatter_dimension=0, tiled=True),
        lax.psum_scatter(grad_key_scale, "dp", scatter_dimension=0, tiled=True),
        lax.psum_scatter(grad_output_weight, "dp", scatter_dimension=1, tiled=True),
        lax.psum_scatter(grad_post_gain, "dp", scatter_dimension=0, tiled=True),
        lax.psum_scatter(grad_feed_gain, "dp", scatter_dimension=0, tiled=True),
        lax.psum_scatter(grad_gate_weight, "dp", scatter_dimension=0, tiled=True),
        lax.psum_scatter(grad_up_weight, "dp", scatter_dimension=0, tiled=True),
        lax.psum_scatter(grad_down, "dp", scatter_dimension=1, tiled=True),
        lax.psum_scatter(grad_final_gain, "dp", scatter_dimension=0, tiled=True),
    )
    return (
        layer_out,
        input_grad,
        summed_all[0],
        summed_all[1],
        summed_all[2],
        summed_all[3],
        summed_all[4],
        summed_all[5],
        summed_all[6],
        summed_all[7],
        summed_all[8],
        summed_all[9],
        summed_all[10],
        summed_all[11],
        summed_all[12],
    )


def solution(mesh):
    in_specs = (
        P("dp", None),
        P("dp", None),
        P("dp"),
        P("dp", "tensor"),
        P("dp", None),
        P("dp", None),
        P("dp"),
        P("dp"),
        P("tensor", "dp"),
        P("dp"),
        P("dp"),
        P("dp", "tensor"),
        P("dp", "tensor"),
        P("tensor", "dp"),
        P("dp"),
    )
    out_specs = (
        P("dp", None),
        P("dp", None),
        P("dp"),
        P("dp", "tensor"),
        P("dp", None),
        P("dp", None),
        P("dp"),
        P("dp"),
        P("tensor", "dp"),
        P("dp"),
        P("dp"),
        P("dp", "tensor"),
        P("dp", "tensor"),
        P("tensor", "dp"),
        P("dp"),
    )
    return jax.shard_map(
        on_device, mesh=mesh, in_specs=in_specs, out_specs=out_specs, check_vma=False
    )
```

profile of v0, /device:TPU:1, one launch (start us, length us, event | category | flops | bytes accessed | tf_op | source)
XLA Modules:
  0.0 1760.3 jit_solution(13789522269199206999)
XLA Ops:
  16.8 142.2 %all-reduce.26 = (bf16[256]{0:T(256)(128)(2,1)S(1)}, bf16[256]{0:T(256)(128)(2,1)S(1)}, bf16[1152]{0:T(1024)(128)(2,1)S(1)}) all-reduce(bf16[256]{0:T(256)(128)(2,1)S(1)} %dynamic-update-slice.1, bf16[256]{0:T(256)(128)(2,1)S(1)} %dynamic-update-slice, bf16[1152]{0:T(1024)(128)(2,1)S(1)} %dynamic-update-slice.2), channel_id=1, replica_groups=mesh['dp'=64,'tensor'=2] {'dp'}, use_global_device_ids=true, to_apply=%add.5 | all-reduce | flops 1664 | bytes 6656
  163.7 59.2 %all-gather.7.cloned.1.call-done = bf16[64,18,1025]{2,1,0:T(8,128)(2,1)} async-done(((bf16[1,18,1025]{2,1,0:T(8,128)(2,1)}), bf16[64,18,1025]{2,1,0:T(8,128)(2,1)}) %all-gather.7.cloned.1.call-update) | async-done | bytes 2361616 | tf_op jit(solution)/shard_map/all_gather | solution.py:16
  222.9 4.3 reshape.328
  241.2 4.9 all-to-all-start
  246.4 54.5 %all-to-all-done = f32[2,256,1152]{2,1,0:T(8,128)} async-done(((f32[2,256,1152]{2,1,0:T(8,128)}), f32[2,256,1152]{2,1,0:T(8,128)}, u32[]{:S(2)}, u32[]{:S(2)}) %all-to-all-start) | async-done | bytes 2359328 | tf_op jit(solution)/shard_map/all_to_all | solution.py:37
  303.5 126.5 %all-gather.11.cloned.1.call-done = bf16[64,18,10370]{2,1,0:T(8,128)(2,1)} async-done(((bf16[1,18,10370]{2,1,0:T(8,128)(2,1)}), bf16[64,18,10370]{2,1,0:T(8,128)(2,1)}) %all-gather.11.cloned.1.call-update) | async-done | bytes 23892496 | tf_op jit(solution)/shard_map/all_gather | solution.py:27
  430.1 28.7 %reshape.332 = bf16[1152,10370]{1,0:T(8,128)(2,1)} reshape(bf16[64,18,10370]{2,1,0:T(8,128)(2,1)} %all-gather.11.cloned.1.call-done) | data formatting | bytes 47784960
  460.3 8.6 fusion.14
  472.0 7.7 multiply_convert_fusion.1
  479.7 5.6 fusion.29
  486.5 19.9 %all_to_all.36 = bf16[2,256,1152]{2,1,0:T(8,128)(2,1)S(1)} all-to-all(bf16[2,256,1152]{2,1,0:T(8,128)(2,1)S(1)} %broadcast_in_dim.106), channel_id=1, replica_groups=mesh['dp'=64,'tensor'=2] {'tensor'}, dimensions={0} | all-to-all | bytes 2359296 | tf_op jit(solution)/shard_map/all_to_all | solution.py:37
  510.3 7.9 fusion.104
  518.2 9.9 fusion.22
  528.1 9.5 fusion.102
  537.6 7.8 fusion.103
  545.4 7.1 fusion.8
  552.5 6.6 fusion.26
  560.3 4.6 all-to-all-start.2
  565.5 31.3 %all-to-all-done.2 = bf16[2,256,1152]{2,1,0:T(8,128)(2,1)} async-done(((bf16[2,256,1152]{2,1,0:T(8,128)(2,1)}), bf16[2,256,1152]{2,1,0:T(8,128)(2,1)}, u32[]{:S(2)}, u32[]{:S(2)}) %all-to-all-start.2) | async-done | bytes 1179680 | tf_op jit(solution)/shard_map/all_to_all | solution.py:37
  608.1 4.1 all-to-all-start.4
  614.8 8.9 all-to-all-done.4
  625.3 4.1 all-to-all-start.5
  634.2 7.3 all-to-all-done.5
  647.4 211.9 %fusion.97 = (f32[24,512]{1,0:T(8,128)}, f32[24,256]{1,0:T(8,128)}, f32[24,256]{1,0:T(8,128)}, f32[512,24]{0,1:T(8,128)S(1)}) fusion(f32[1152,512]{1,0:T(8,128)S(1)} %fusion.92, f32[1152,256]{1,0:T(8,128)} %fusion.90, f32[1152,256]{1,0:T(8,128)} %fusion.88, f32[512,1152]{0,1:T(8,128)} %fusion.101), kind=kCustom, calls=%all-reduce-scatter.4 | all-reduce-scatter fusion | flops 2359297 | bytes 7225856
  862.7 5.4 collective-permute-start.29
  868.8 7.7 collective-permute-start.31
  880.4 6.1 collective-permute-start.25
  886.6 4.0 collective-permute-start.24
  892.0 4.0 collective-permute-start.22
  897.6 4.2 collective-permute-start.20
  903.2 4.3 collective-permute-start.18
  910.1 3.5 collective-permute-start.16
  934.2 3.7 collective-permute-start.36
  945.0 3.4 collective-permute-start.33
  948.4 3.7 collective-permute-start.32
  968.0 6.1 collective-permute-start.6
  977.3 3.2 all-to-all-start.6
  981.8 3.7 collective-permute-start.3
  997.2 4.9 all-to-all-start.3
  1005.7 4.3 collective-permute-start.61
  1016.4 13.0 concatenate.19
  1029.4 3.4 collective-permute-start.57
  1042.5 12.2 concatenate.20
  1061.5 3.5 collective-permute-start.49
  1068.2 6.7 concatenate.18
  1074.9 23.8 %concatenate.21 = f32[512,402]{0,1:T(8,128)} concatenate(f32[512,18]{0,1:T(8,128)S(1)} %collective-permute-done.63, f32[512,24]{0,1:T(8,128)} %copy-done.56, f32[512,24]{0,1:T(8,128)} %copy-done.57, f32[512,24]{0,1:T(8,128)} %collective-permute-done.60, f32[512,24]{0,1:T(8,128)} %collective-permute-done.59, f32[512,24]{0,1:T(8,128)} %collective-permute-done.58, ...), dimensions={1} | concatenate | bytes 1646592
  1104.8 274.0 %all-reduce.24 = (f32[1152]{0:T(1024)S(1)}, f32[256]{0:T(256)S(1)}, f32[256]{0:T(256)S(1)}, f32[1152]{0:T(1024)S(1)}, f32[1152]{0:T(1024)S(1)}, /*index=5*/f32[1152]{0:T(1024)S(1)}) all-reduce(f32[1152]{0:T(1024)S(1)} %get-tuple-element.68, f32[256]{0:T(256)S(1)} %convert_reduce_fusion.7, ...), channel_id=2, replica_groups=mesh['dp'=64,'tensor'=2] {'dp'}, use_global_device_ids=true, to_apply=%region_22.23.clone | all-reduce | flops 5120 | bytes 40960
  1383.7 366.0 %all-reduce.30.cloned.1.call-done = (f32[1152,3456]{1,0:T(8,128)}, f32[1152,3456]{1,0:T(8,128)}, f32[3456,1152]{0,1:T(8,128)}) async-done(((f32[1152,3456]{1,0:T(8,128)}, f32[1152,3456]{1,0:T(8,128)}, f32[3456,1152]{0,1:T(8,128)}), (f32[1152,3456]{1,0:T(8,128)}, f32[1152,3456]{1,0:T(8,128)}, f32[3456,1152]{0,1:T(8,128)})) %all-reduce.30.cloned.1.call-update) | async-done | bytes 47775760
  (471 shorter events, 182.5 us)
Async XLA Ops:
  7.2 153.3 %all-gather.9.cloned.1.call-start = ((), (), s32[]{:S(2)}) async-start(), calls=%async_computation.8 | async-start | bytes 1597440 | tf_op jit(solution)/shard_map/all_gather | solution.py:130
  8.0 214.9 %all-gather.7.cloned.1.call-start = ((), (), s32[]{:S(2)}) async-start(), calls=%async_computation.7 | async-start | bytes 3594240 | tf_op jit(solution)/shard_map/all_gather | solution.py:16
  10.3 419.8 %all-gather.11.cloned.1.call-start = ((), (), s32[]{:S(2)}) async-start(), calls=%async_computation.9 | async-start | bytes 32747520 | tf_op jit(solution)/shard_map/all_gather | solution.py:27
  241.2 59.7 %all-to-all-start = ((f32[2,256,1152]{2,1,0:T(8,128)}), f32[2,256,1152]{2,1,0:T(8,128)}, u32[]{:S(2)}, u32[]{:S(2)}) async-start(f32[2,256,1152]{2,1,0:T(8,128)} %broadcast_in_dim.105), calls=%async_computation | async-start | bytes 4718592 | tf_op jit(solution)/shard_map/all_to_all | solution.py:37
  246.1 1503.6 %all-reduce.30.cloned.1.call-start = ((), (), s32[]{:S(2)}) async-start(), calls=%async_computation.10 | async-start | bytes 95551488
  560.3 36.5 %all-to-all-start.2 = ((bf16[2,256,1152]{2,1,0:T(8,128)(2,1)}), bf16[2,256,1152]{2,1,0:T(8,128)(2,1)}, u32[]{:S(2)}, u32[]{:S(2)}) async-start(bf16[2,256,1152]{2,1,0:T(8,128)(2,1)} %broadcast_in_dim.108), calls=%async_computation.2 | async-start | bytes 2359296 | tf_op jit(solution)/shard_map/all_to_all | solution.py:37
  608.1 15.6 all-to-all-start.4
  625.3 16.2 all-to-all-start.5
  860.1 17.7 %collective-permute-start.47 = (f32[18,256]{1,0:T(8,128)S(1)}, f32[18,256]{1,0:T(8,128)S(1)}, u32[]{:S(2)}, u32[]{:S(2)}) collective-permute-start(f32[18,256]{1,0:T(8,128)S(1)} %slice.67), channel_id=1, source_target_pairs={{0,32},{2,34},{4,36},{6,38},{8,40},{10,42},{12,44},{14,46},{16,48}... | collective-permute-start | bytes 55304
  861.4 19.1 %collective-permute-start.30 = (f32[24,256]{1,0:T(8,128)}, f32[24,256]{1,0:T(8,128)S(1)}, u32[]{:S(2)}, u32[]{:S(2)}) collective-permute-start(f32[24,256]{1,0:T(8,128)} %get-tuple-element.91), channel_id=1, source_target_pairs={{0,30},{2,32},{4,34},{6,36},{8,38},{10,40},{12,42},{14,44},{16,46}... | collective-permute-start | bytes 73736
  862.7 23.9 %collective-permute-start.29 = (f32[24,256]{1,0:T(8,128)}, f32[24,256]{1,0:T(8,128)S(1)}, u32[]{:S(2)}, u32[]{:S(2)}) collective-permute-start(f32[24,256]{1,0:T(8,128)} %get-tuple-element.91), channel_id=1, source_target_pairs={{0,28},{2,30},{4,32},{6,34},{8,36},{10,38},{12,40},{14,42},{16,44}... | collective-permute-start | bytes 73736
  876.5 14.1 collective-permute-start.28
  877.8 14.2 collective-permute-start.27
  879.1 16.9 collective-permute-start.26
  880.4 17.2 collective-permute-start.25
  886.6 15.3 collective-permute-start.24
  892.0 15.5 collective-permute-start.22
  896.0 14.0 collective-permute-start.21
  897.6 15.9 collective-permute-start.20
  903.2 13.9 collective-permute-start.18
  940.1 17.5 collective-permute-start.63
  941.5 17.4 collective-permute-start.15
  958.9 15.2 collective-permute-start.10
  961.2 19.3 %collective-permute-start.9 = (f32[24,512]{1,0:T(8,128)}, f32[24,512]{1,0:T(8,128)S(1)}, u32[]{:S(2)}, u32[]{:S(2)}) collective-permute-start(f32[24,512]{1,0:T(8,128)} %get-tuple-element.90), channel_id=1, source_target_pairs={{0,20},{2,22},{4,24},{6,26},{8,28},{10,30},{12,32},{14,34},{16,36}... | collective-permute-start | bytes 147464
  964.0 17.8 %collective-permute-start.8 = (f32[24,512]{1,0:T(8,128)}, f32[24,512]{1,0:T(8,128)S(1)}, u32[]{:S(2)}, u32[]{:S(2)}) collective-permute-start(f32[24,512]{1,0:T(8,128)} %get-tuple-element.90), channel_id=1, source_target_pairs={{0,18},{2,20},{4,22},{6,24},{8,26},{10,28},{12,30},{14,32},{16,34}... | collective-permute-start | bytes 147464
  966.2 19.4 %collective-permute-start.7 = (f32[24,512]{1,0:T(8,128)}, f32[24,512]{1,0:T(8,128)S(1)}, u32[]{:S(2)}, u32[]{:S(2)}) collective-permute-start(f32[24,512]{1,0:T(8,128)} %get-tuple-element.90), channel_id=1, source_target_pairs={{0,16},{2,18},{4,20},{6,22},{8,24},{10,26},{12,28},{14,30},{16,32}... | collective-permute-start | bytes 147464
  968.0 18.9 %collective-permute-start.6 = (f32[24,512]{1,0:T(8,128)}, f32[24,512]{1,0:T(8,128)S(1)}, u32[]{:S(2)}, u32[]{:S(2)}) collective-permute-start(f32[24,512]{1,0:T(8,128)} %get-tuple-element.90), channel_id=1, source_target_pairs={{0,14},{2,16},{4,18},{6,20},{8,22},{10,24},{12,26},{14,28},{16,30}... | collective-permute-start | bytes 147464
  974.2 15.9 collective-permute-start.5
  977.3 18.8 %all-to-all-start.6 = ((bf16[2,2,128]{2,1,0:T(2,128)(2,1)}), bf16[2,2,128]{2,1,0:T(2,128)(2,1)S(1)}, u32[]{:S(2)}, u32[]{:S(2)}) async-start(bf16[2,2,128]{2,1,0:T(2,128)(2,1)} %reshape.361), calls=%async_computation.6 | async-start | bytes 2048 | tf_op jit(solution)/shard_map/all_to_all | solution.py:37
  980.5 23.7 %collective-permute-start.4 = (f32[24,512]{1,0:T(8,128)}, f32[24,512]{1,0:T(8,128)S(1)}, u32[]{:S(2)}, u32[]{:S(2)}) collective-permute-start(f32[24,512]{1,0:T(8,128)} %get-tuple-element.90), channel_id=1, source_target_pairs={{0,10},{2,12},{4,14},{6,16},{8,18},{10,20},{12,22},{14,24},{16,26}... | collective-permute-start | bytes 147464
  981.8 23.8 %collective-permute-start.3 = (f32[24,512]{1,0:T(8,128)}, f32[24,512]{1,0:T(8,128)S(1)}, u32[]{:S(2)}, u32[]{:S(2)}) collective-permute-start(f32[24,512]{1,0:T(8,128)} %get-tuple-element.90), channel_id=1, source_target_pairs={{0,8},{2,10},{4,12},{6,14},{8,16},{10,18},{12,20},{14,22},{16,24},... | collective-permute-start | bytes 147464
  985.6 24.4 %collective-permute-start.2 = (f32[24,512]{1,0:T(8,128)}, f32[24,512]{1,0:T(8,128)S(1)}, u32[]{:S(2)}, u32[]{:S(2)}) collective-permute-start(f32[24,512]{1,0:T(8,128)} %get-tuple-element.90), channel_id=1, source_target_pairs={{0,6},{2,8},{4,10},{6,12},{8,14},{10,16},{12,18},{14,20},{16,22},{... | collective-permute-start | bytes 147464
  986.9 25.2 %collective-permute-start.1 = (f32[24,512]{1,0:T(8,128)}, f32[24,512]{1,0:T(8,128)S(1)}, u32[]{:S(2)}, u32[]{:S(2)}) collective-permute-start(f32[24,512]{1,0:T(8,128)} %get-tuple-element.90), channel_id=1, source_target_pairs={{0,4},{2,6},{4,8},{6,10},{8,12},{10,14},{12,16},{14,18},{16,20},{1... | collective-permute-start | bytes 147464
  990.7 23.3 %collective-permute-start = (f32[24,512]{1,0:T(8,128)}, f32[24,512]{1,0:T(8,128)S(1)}, u32[]{:S(2)}, u32[]{:S(2)}) collective-permute-start(f32[24,512]{1,0:T(8,128)} %get-tuple-element.90), channel_id=1, source_target_pairs={{0,2},{2,4},{4,6},{6,8},{8,10},{10,12},{12,14},{14,16},{16,18},{18... | collective-permute-start | bytes 147464
  997.2 103.6 %all-to-all-start.3 = ((bf16[2,256,1152]{2,1,0:T(8,128)(2,1)}), bf16[2,256,1152]{2,1,0:T(8,128)(2,1)S(1)}, u32[]{:S(2)}, u32[]{:S(2)}) async-start(bf16[2,256,1152]{2,1,0:T(8,128)(2,1)} %broadcast_in_dim.112), calls=%async_computation.3 | async-start | bytes 2359296 | tf_op jit(solution)/shard_map/all_to_all | solution.py:37
  1004.2 25.2 %collective-permute-start.62 = (f32[512,24]{0,1:T(8,128)S(1)}, f32[512,24]{0,1:T(8,128)S(1)}, u32[]{:S(2)}, u32[]{:S(2)}) collective-permute-start(f32[512,24]{0,1:T(8,128)S(1)} %get-tuple-element.93), channel_id=1, source_target_pairs={{0,30},{2,32},{4,34},{6,36},{8,38},{10,40},{12,42},{14,44},{16,46}... | collective-permute-start | bytes 147464
  1005.7 27.2 %collective-permute-start.61 = (f32[512,24]{0,1:T(8,128)S(1)}, f32[512,24]{0,1:T(8,128)S(1)}, u32[]{:S(2)}, u32[]{:S(2)}) collective-permute-start(f32[512,24]{0,1:T(8,128)S(1)} %get-tuple-element.93), channel_id=1, source_target_pairs={{0,28},{2,30},{4,32},{6,34},{8,36},{10,38},{12,40},{14,42},{16,44}... | collective-permute-start | bytes 147464
  1010.0 25.3 %collective-permute-start.60 = (f32[512,24]{0,1:T(8,128)S(1)}, f32[512,24]{0,1:T(8,128)}, u32[]{:S(2)}, u32[]{:S(2)}) collective-permute-start(f32[512,24]{0,1:T(8,128)S(1)} %get-tuple-element.93), channel_id=1, source_target_pairs={{0,26},{2,28},{4,30},{6,32},{8,34},{10,36},{12,38},{14,40},{16,42}... | collective-permute-start | bytes 147464
  1012.2 25.7 %collective-permute-start.59 = (f32[512,24]{0,1:T(8,128)S(1)}, f32[512,24]{0,1:T(8,128)}, u32[]{:S(2)}, u32[]{:S(2)}) collective-permute-start(f32[512,24]{0,1:T(8,128)S(1)} %get-tuple-element.93), channel_id=1, source_target_pairs={{0,24},{2,26},{4,28},{6,30},{8,32},{10,34},{12,36},{14,38},{16,40}... | collective-permute-start | bytes 147464
  1014.1 25.9 %collective-permute-start.58 = (f32[512,24]{0,1:T(8,128)S(1)}, f32[512,24]{0,1:T(8,128)}, u32[]{:S(2)}, u32[]{:S(2)}) collective-permute-start(f32[512,24]{0,1:T(8,128)S(1)} %get-tuple-element.93), channel_id=1, source_target_pairs={{0,22},{2,24},{4,26},{6,28},{8,30},{10,32},{12,34},{14,36},{16,38}... | collective-permute-start | bytes 147464
  1029.4 25.3 %collective-permute-start.57 = (f32[512,24]{0,1:T(8,128)S(1)}, f32[512,24]{0,1:T(8,128)}, u32[]{:S(2)}, u32[]{:S(2)}) collective-permute-start(f32[512,24]{0,1:T(8,128)S(1)} %get-tuple-element.93), channel_id=1, source_target_pairs={{0,20},{2,22},{4,24},{6,26},{8,28},{10,30},{12,32},{14,34},{16,36}... | collective-permute-start | bytes 147464
  1032.8 24.9 %collective-permute-start.56 = (f32[512,24]{0,1:T(8,128)S(1)}, f32[512,24]{0,1:T(8,128)}, u32[]{:S(2)}, u32[]{:S(2)}) collective-permute-start(f32[512,24]{0,1:T(8,128)S(1)} %get-tuple-element.93), channel_id=1, source_target_pairs={{0,18},{2,20},{4,22},{6,24},{8,26},{10,28},{12,30},{14,32},{16,34}... | collective-permute-start | bytes 147464
  1035.4 24.2 %collective-permute-start.55 = (f32[512,24]{0,1:T(8,128)S(1)}, f32[512,24]{0,1:T(8,128)}, u32[]{:S(2)}, u32[]{:S(2)}) collective-permute-start(f32[512,24]{0,1:T(8,128)S(1)} %get-tuple-element.93), channel_id=1, source_target_pairs={{0,16},{2,18},{4,20},{6,22},{8,24},{10,26},{12,28},{14,30},{16,32}... | collective-permute-start | bytes 147464
  1037.8 23.7 %collective-permute-start.54 = (f32[512,24]{0,1:T(8,128)S(1)}, f32[512,24]{0,1:T(8,128)}, u32[]{:S(2)}, u32[]{:S(2)}) collective-permute-start(f32[512,24]{0,1:T(8,128)S(1)} %get-tuple-element.93), channel_id=1, source_target_pairs={{0,14},{2,16},{4,18},{6,20},{8,22},{10,24},{12,26},{14,28},{16,30}... | collective-permute-start | bytes 147464
  1040.0 25.0 %collective-permute-start.53 = (f32[512,24]{0,1:T(8,128)S(1)}, f32[512,24]{0,1:T(8,128)}, u32[]{:S(2)}, u32[]{:S(2)}) collective-permute-start(f32[512,24]{0,1:T(8,128)S(1)} %get-tuple-element.93), channel_id=1, source_target_pairs={{0,12},{2,14},{4,16},{6,18},{8,20},{10,22},{12,24},{14,26},{16,28}... | collective-permute-start | bytes 147464
  1054.7 20.1 %collective-permute-start.52 = (f32[512,24]{0,1:T(8,128)S(1)}, f32[512,24]{0,1:T(8,128)}, u32[]{:S(2)}, u32[]{:S(2)}) collective-permute-start(f32[512,24]{0,1:T(8,128)S(1)} %get-tuple-element.93), channel_id=1, source_target_pairs={{0,10},{2,12},{4,14},{6,16},{8,18},{10,20},{12,22},{14,24},{16,26}... | collective-permute-start | bytes 147464
  1057.7 17.2 collective-permute-start.51
  1059.6 15.3 collective-permute-start.50
  (143 other events, 4421.5 us)
Sparse Core Ops, SparseCore 0:
  9.8 106.2 all-gather.8
  118.4 104.4 all-gather.6
  225.2 204.8 all-gather.10
  545.5 1204.1 all-reduce.29
where the time goes:
time: 1780 us; the launch traced here: 1760 us
  waiting for transfers between devices  655 us (37%)
  blocking collectives  648 us (36%)
  starting transfers between devices  189 us (11%)
  local copies, waits for them, and re-layouts  133 us (7%)
  matrix products  93.1 us (5%)
  other arithmetic  22.6 us (1%)
  between operations  19.8 us (1%)
    unnamed x3, blocking collectives  628 us
    unnamed x69, waiting for transfers between devices  367 us
    unnamed x65, starting transfers between devices  163 us
    all_gather x1, waiting for transfers between devices, rows_first(): out, at, outs = (lax.all_gather(both, axis, axis=0, tiled=True), 0, [])  127 us
    unnamed x266, local copies, waits for them, and re-layouts  118 us
    all_to_all x6, waiting for transfers between devices, from_everyone(): return lax.all_to_all(copies, axis, split_axis=0, concat_axis=0, tiled=True)  102 us
    all_gather x1, waiting for transfers between devices, sent_together(): out, at, outs = (lax.all_gather(both, axis, axis=dim, tiled=True), 0, [])  59.2 us
  transfers between devices with their start and end apart: 74, of which 7 were waited for; matrix products, arithmetic and copies ran while one was open for 20% of the time, Pallas kernels for 0%

commit v1 on v0

v1 whole, which is shorter than its diff:
```python
import jax
import jax.numpy as jnp
import numpy as np
from jax import lax
from jax.sharding import Mesh, PartitionSpec as P

D = 1152
HD = 256
SEQ = 256
HALF = SEQ // 2
UNITS = 864
PAD = 896
EPS = 1e-06
THETA = 1000000.0
SCALE = HD ** (-0.5)
BF = jnp.bfloat16
F32 = jnp.float32
PLANE = ("y", "x")


def swap(field, axes, mask, size):
    return lax.ppermute(field, axes, [(i, i ^ mask) for i in range(size)])


def across(field, mask):
    return swap(field, ("zl", "t"), mask, 4)


def other_core(field):
    return swap(field, "c", 1, 2)


def other_member(field):
    return swap(field, "t", 1, 2)


def column_gather(block):
    same = jnp.concatenate([block] + [across(block, m) for m in (1, 2, 3)], axis=0)
    return jnp.concatenate([same, other_core(same)], axis=0)


def column_sum(parts):
    half = parts.shape[0] // 2
    low = parts.astype(BF)
    mine = (low[:half].astype(F32) + other_core(low[half:]).astype(F32)).astype(BF)
    rows = half // 4
    total = mine[:rows].astype(F32)
    for m in (1, 2, 3):
        total = total + across(mine[m * rows : (m + 1) * rows], m).astype(F32)
    return total


def product(left, right):
    return jnp.dot(left, right, preferred_element_type=F32)


def contract_rows(left, right):
    return lax.dot_general(left, right, (((0,), (0,)), ((), ())), preferred_element_type=F32)


def contract_cols(left, right):
    return lax.dot_general(left, right, (((1,), (1,)), ((), ())), preferred_element_type=F32)


def inverse_rms(field):
    return lax.rsqrt(jnp.mean(field * field, axis=-1, keepdims=True) + EPS)


def norm_back(grad, field, inv, gain):
    scaled = grad * gain
    back = inv * scaled - field * (inv * inv * inv) * jnp.mean(field * scaled, axis=-1, keepdims=True)
    return back, grad * field * inv


def tables():
    half = HD // 2
    freq = np.float32(THETA) ** (-np.arange(half, dtype=np.float32) / np.float32(half))
    angle = np.arange(SEQ, dtype=np.float32)[:, None] * freq[None, :].astype(np.float32)
    return jnp.asarray(np.cos(angle).astype(np.float32)), jnp.asarray(np.sin(angle).astype(np.float32))


def rotate(field, cosine, sine):
    half = HD // 2
    first, second = field[..., :half], field[..., half:]
    return jnp.concatenate([first * cosine - second * sine, second * cosine + first * sine], axis=-1)


def quarters(weight):
    cut = weight.reshape(weight.shape[0], 4, UNITS).transpose(1, 0, 2)
    return jnp.pad(cut, ((0, 0), (0, 0), (0, PAD - UNITS)))


def whole_units(block):
    return block[:, :, :UNITS].transpose(1, 0, 2).reshape(block.shape[1], 4 * UNITS)


def on_device(
    tokens,
    cotangent,
    input_gain,
    query_weight,
    key_weight,
    value_weight,
    query_gain,
    key_gain,
    output_weight,
    attention_gain,
    feed_gain,
    gate_weight,
    up_weight,
    down_weight,
    output_gain,
):
    core = lax.axis_index("c")
    member = lax.axis_index("t")
    shard = input_gain.shape[0]
    heads_gain = jnp.concatenate([query_gain, key_gain, jnp.zeros((shard - 8,), BF)])
    gains = jnp.stack([input_gain, attention_gain, feed_gain, output_gain, heads_gain], axis=1)
    gains = jnp.pad(gains, ((0, 0), (0, 123)))
    half0 = jnp.concatenate([query_weight, key_weight, gains], axis=1)
    half1 = jnp.concatenate([value_weight, output_weight.T, gains], axis=1)
    pack = jnp.concatenate(
        [
            jnp.stack([half0, half1, half0, half1]),
            quarters(gate_weight),
            quarters(up_weight),
            quarters(down_weight.T),
        ],
        axis=2,
    )
    got = lax.all_to_all(pack, ("zl", "c"), 0, 0, tiled=True).reshape(4 * shard, -1)
    att_shard = got[:, :PAD]
    att_half = lax.all_to_all(
        jnp.broadcast_to(att_shard[None], (16, *att_shard.shape)), PLANE, 0, 0, tiled=True
    ).reshape(D, PAD)
    feed_weights = lax.all_gather(got[:, PAD:], PLANE, axis=0, tiled=True)

    gain_cols = att_half[:, 768:773].astype(F32).T
    norm_gain, post_gain, feed_scale, final_gain = (gain_cols[i][None, :] for i in range(4))
    head_cols = gain_cols[4].reshape(64, shard)
    query_scale = head_cols[:, :4].reshape(1, HD)
    key_scale = head_cols[:, 4:8].reshape(1, HD)
    own_half = att_half[:, :768]
    their_half = other_core(own_half)
    first_half = jnp.where(core == 0, own_half, their_half)
    second_half = jnp.where(core == 0, their_half, own_half)
    cosine, sine = tables()

    rows = tokens.astype(F32)
    inv_in = inverse_rms(rows)
    normed = (rows * inv_in * norm_gain).astype(BF)
    qk = product(normed, first_half)
    queries = jnp.stack([qk[:, :HD], qk[:, HD : 2 * HD]])
    keys = qk[:, 2 * HD :]
    values = product(normed, second_half[:, :HD]).astype(BF)
    inv_q = inverse_rms(queries)
    inv_k = inverse_rms(keys)
    q_rot = rotate(queries * inv_q * query_scale, cosine, sine).astype(BF)
    k_rot = rotate(keys * inv_k * key_scale, cosine, sine).astype(BF)
    scores = jnp.einsum("hqd,kd->hqk", q_rot, k_rot, preferred_element_type=F32) * SCALE
    causal = jnp.arange(SEQ)[None, :] <= jnp.arange(SEQ)[:, None]
    scores = jnp.where(causal, scores, -1e30)
    expo = jnp.exp(scores - jnp.max(scores, axis=-1, keepdims=True))
    probs_f = expo / jnp.sum(expo, axis=-1, keepdims=True)
    probs = probs_f.astype(BF)
    mixed_heads = jnp.einsum("hqk,kd->hqd", probs, values, preferred_element_type=F32).astype(BF)
    mixed = jnp.concatenate([mixed_heads[0], mixed_heads[1]], axis=1)
    output_t = second_half[:, HD:]
    branch_part = contract_cols(mixed, output_t)

    def my_half(field):
        return lax.dynamic_slice_in_dim(field, member * HALF, HALF, 0)

    def their_rows(field):
        return lax.dynamic_slice_in_dim(field, (1 - member) * HALF, HALF, 0)

    def whole_rows(field):
        theirs = other_member(field)
        top = jnp.where(member == 0, field, theirs)
        bottom = jnp.where(member == 0, theirs, field)
        return jnp.concatenate([top, bottom], axis=0)

    branch = my_half(branch_part) + other_member(their_rows(branch_part).astype(BF)).astype(F32)
    my_rows = my_half(tokens).astype(F32)
    inv_b = inverse_rms(branch)
    hidden = my_rows + branch * inv_b * post_gain
    inv_h = inverse_rms(hidden)
    feed = (hidden * inv_h * feed_scale).astype(BF)

    all_feed = column_gather(feed)
    gate_up = feed_weights[:, : 2 * PAD]
    down_t = feed_weights[:, 2 * PAD :]
    both = product(all_feed, gate_up)
    gate, upper = both[:, :PAD], both[:, PAD:]
    k0 = np.float32(np.sqrt(2.0 / np.pi))
    square = gate * gate
    tanh = jnp.tanh(k0 * gate * (1.0 + 0.044715 * square))
    gelu = 0.5 * gate * (1.0 + tanh)
    slope = 0.5 * (1.0 + tanh) + 0.5 * gate * (1.0 - tanh * tanh) * (k0 * (1.0 + 3 * 0.044715 * square))
    activ = (gelu * upper).astype(BF)
    second = column_sum(contract_cols(activ, down_t))
    inv_s = inverse_rms(second)
    layer_half = (hidden + second * inv_s * final_gain).astype(BF)
    layer_out = whole_rows(layer_half)

    upstream = my_half(cotangent).astype(F32)
    grad_second, final_terms = norm_back(upstream, second, inv_s, final_gain)
    all_grad = column_gather(grad_second.astype(BF))
    grad_activ = product(all_grad, down_t)
    grad_gate = (grad_activ * upper * slope).astype(BF)
    grad_upper = (grad_activ * gelu).astype(BF)
    grad_both = jnp.concatenate([grad_gate, grad_upper], axis=1)
    feed_back = column_sum(contract_cols(grad_both, gate_up))
    ffn_grads = jnp.concatenate(
        [contract_rows(all_feed, grad_both).astype(BF), contract_rows(all_grad, activ).astype(BF)], axis=1
    )
    ffn_sums = lax.psum_scatter(ffn_grads, PLANE, scatter_dimension=0, tiled=True)
    ffn_sums = lax.all_to_all(ffn_sums.reshape(4, shard, 3 * PAD), ("zl", "c"), 0, 0, tiled=True).astype(F32)
    grad_gate_weight = whole_units(ffn_sums[:, :, :PAD])
    grad_up_weight = whole_units(ffn_sums[:, :, PAD : 2 * PAD])
    grad_down = whole_units(ffn_sums[:, :, 2 * PAD :]).T

    hidden_add, feed_terms = norm_back(feed_back, hidden, inv_h, feed_scale)
    grad_hidden = upstream + hidden_add
    grad_branch, post_terms = norm_back(grad_hidden, branch, inv_b, post_gain)
    grad_branch = whole_rows(grad_branch.astype(BF))
    add_all = whole_rows(hidden_add.astype(BF)).astype(F32)
    grad_hidden_all = cotangent.astype(F32) + add_all
    half_gains = jnp.stack([jnp.sum(terms, axis=0) for terms in (post_terms, feed_terms, final_terms)])
    half_gains = half_gains + other_member(half_gains)

    grad_output_t = contract_rows(grad_branch, mixed)
    grad_mixed = product(grad_branch, output_t).astype(BF)
    gm = jnp.stack([grad_mixed[:, :HD], grad_mixed[:, HD:]])
    grad_probs = jnp.einsum("hqd,kd->hqk", gm, values, preferred_element_type=F32)
    center = jnp.sum(probs_f * grad_probs, axis=-1, keepdims=True)
    grad_scores = (probs_f * (grad_probs - center)).astype(BF)
    grad_krot = jnp.einsum("hqk,hqd->kd", grad_scores, q_rot, preferred_element_type=F32) * SCALE
    grad_values = jnp.einsum("hqk,hqd->kd", probs, gm, preferred_element_type=F32)
    kv_part = jnp.concatenate([grad_krot, grad_values], axis=1).astype(BF)
    kv = kv_part.astype(F32) + other_member(kv_part).astype(F32)

    grad_qrot = jnp.einsum("hqk,kd->hqd", grad_scores, k_rot, preferred_element_type=F32) * SCALE
    grad_queries, query_terms = norm_back(rotate(grad_qrot, cosine, -sine), queries, inv_q, query_scale)
    query_gain_part = jnp.sum(query_terms, axis=(0, 1))
    query_gain_sum = query_gain_part + other_member(query_gain_part)
    grad_queries = grad_queries.astype(BF)
    grad_q = jnp.concatenate([grad_queries[0], grad_queries[1]], axis=1)
    normed_part = contract_cols(grad_q, first_half[:, : 2 * HD]).astype(BF)
    normed_q = normed_part.astype(F32) + other_member(normed_part).astype(F32)

    grad_keys, key_terms = norm_back(rotate(kv[:, :HD], cosine, -sine), keys, inv_k, key_scale)
    key_gain_sum = jnp.sum(key_terms, axis=0)
    grad_keys = grad_keys.astype(BF)
    grad_values_low = kv[:, HD:].astype(BF)
    grad_normed = (
        normed_q
        + contract_cols(grad_keys, first_half[:, 2 * HD :])
        + contract_cols(grad_values_low, second_half[:, :HD])
    )
    input_add, input_terms = norm_back(grad_normed, rows, inv_in, norm_gain)
    input_grad = grad_hidden_all + input_add
    input_gain_sum = jnp.sum(input_terms, axis=0)

    grad_qk = contract_rows(normed, jnp.concatenate([grad_q, grad_keys], axis=1)).astype(BF)
    grad_v = contract_rows(normed, grad_values_low).astype(BF)
    head_sums = jnp.pad(
        jnp.concatenate([query_gain_sum.reshape(64, 4), key_gain_sum.reshape(64, 4)], axis=1),
        ((0, 0), (0, shard - 8)),
    ).reshape(1, D)
    gain_sums = jnp.concatenate([input_gain_sum[None], half_gains, head_sums], axis=0).T
    gain_sums = jnp.pad(gain_sums.astype(BF), ((0, 0), (0, 123)))
    side0 = jnp.concatenate([grad_qk, gain_sums], axis=1)
    side1 = jnp.concatenate([grad_v, grad_output_t.astype(BF), jnp.zeros((D, 128), BF)], axis=1)
    keep = jnp.where(core == 0, side0, side1)
    give = jnp.where(core == 0, side1, side0)
    att_sums = (keep.astype(F32) + other_core(give).astype(F32)).astype(BF)
    att_sums = lax.all_to_all(att_sums.reshape(16, 4 * shard, PAD), PLANE, 0, 0, tiled=True)
    att_sums = jnp.sum(att_sums.astype(F32), axis=0).astype(BF)
    att_sums = lax.all_to_all(att_sums.reshape(4, shard, PAD), ("zl", "c"), 0, 0, tiled=True).astype(F32)
    out0 = att_sums[0] + att_sums[2]
    out1 = att_sums[1] + att_sums[3]
    return (
        layer_out,
        input_grad,
        out0[:, 768],
        out0[:, :512],
        out0[:, 512:768],
        out1[:, :256],
        out0[:4, 772],
        out0[4:8, 772],
        out1[:, 256:768].T,
        out0[:, 769],
        out0[:, 770],
        grad_gate_weight,
        grad_up_weight,
        grad_down,
        out0[:, 771],
    )


def solution(mesh):
    fine = Mesh(mesh.devices.reshape(4, 4, 2, 2, 2), ("y", "x", "zl", "c", "t"))
    dp = ("y", "x", "zl", "c")
    in_specs = (
        P(dp, None),
        P(dp, None),
        P(dp),
        P(dp, "t"),
        P(dp, None),
        P(dp, None),
        P(dp),
        P(dp),
        P("t", dp),
        P(dp),
        P(dp),
        P(dp, "t"),
        P(dp, "t"),
        P("t", dp),
        P(dp),
    )
    out_specs = (
        P(dp, None),
        P(dp, None),
        P(dp),
        P(dp, "t"),
        P(dp, None),
        P(dp, None),
        P(dp),
        P(dp),
        P("t", dp),
        P(dp),
        P(dp),
        P(dp, "t"),
        P(dp, "t"),
        P("t", dp),
        P(dp),
    )
    return jax.shard_map(
        on_device, mesh=fine, in_specs=in_specs, out_specs=out_specs, check_vma=False
    )
```

time: 1780 us -> 393 us (0.22)
  blocking collectives: 648 us -> 54.4 us
  waiting for transfers between devices: 655 us -> 104 us
  starting transfers between devices: 189 us -> 62.5 us
  local copies, waits for them, and re-layouts: 133 us -> 46.1 us
  matrix products: 93.1 us -> 57.5 us
  other arithmetic: 22.6 us -> 50.8 us
    unnamed x3 -> x0, blocking collectives: 628 us -> none
    unnamed x69 -> x3, waiting for transfers between devices: 367 us -> 0.03 us
    all_gather x3 -> x1, waiting for transfers between devices: 186 us -> 0.01 us  [on_device(): feed_weights = lax.all_gather(got[:, PAD:], PLANE, axis=0, tiled=True)]
    unnamed x65 -> x1, starting transfers between devices: 163 us -> 0.04 us
    unnamed x266 -> x184, local copies, waits for them, and re-layouts: 118 us -> 11 us
    ppermute x0 -> x26, waiting for transfers between devices: none -> 80.7 us  [swap(): return lax.ppermute(field, axes, [(i, i ^ mask) for i in range(size)])]
    all_to_all x6 -> x3, waiting for transfers between devices: 102 us -> 22.8 us  [the longest x1 15.1 us: on_device(): lax.all_to_all(att_sums.reshape(16, 4 * shard, PAD), PLANE, 0, 0, tiled=T...]
    ppermute x0 -> x26, starting transfers between devices: none -> 49.5 us  [swap(): return lax.ppermute(field, axes, [(i, i ^ mask) for i in range(size)])]
  transfers between devices with their start and end apart: 74 -> 31, of which waited for: 7 -> 20; matrix products, arithmetic and copies ran while one was open for 20% -> 26% of each run, Pallas kernels for 0% -> 0%
where the time goes in v1:
time: 393 us; the launch traced here: 391 us
  waiting for transfers between devices  104 us (26%)
  starting transfers between devices  62.5 us (16%)
  matrix products  57.5 us (15%)
  blocking collectives  54.4 us (14%)
  other arithmetic  50.8 us (13%)
  local copies, waits for them, and re-layouts  46.1 us (12%)
  between operations  15.7 us (4%)
    ppermute x26, waiting for transfers between devices, swap(): return lax.ppermute(field, axes, [(i, i ^ mask) for i in range(size)])  80.7 us
    ppermute x26, starting transfers between devices, swap(): return lax.ppermute(field, axes, [(i, i ^ mask) for i in range(size)])  49.5 us
    all_to_all x1, blocking collectives, on_device(): lax.all_to_all(jnp.broadcast_to(att_shard[None], (16, *att_shard.shape)),...  39.9 us
    dot_general x5, matrix products, product(): return jnp.dot(left, right, preferred_element_type=F32)  18.6 us
    dot_general x6, matrix products, contract_cols(): lax.dot_general(left, right, (((1,), (1,)), ((), ())), preferred_element_...  17.5 us
    all_to_all x1, waiting for transfers between devices, on_device(): lax.all_to_all(att_sums.reshape(16, 4 * shard, PAD), PLANE, 0, 0, tiled=T...  15.1 us
    dot_general x5, matrix products, contract_rows(): lax.dot_general(left, right, (((0,), (0,)), ((), ())), preferred_element_...  14.9 us
    all_to_all x1, blocking collectives, on_device(): lax.all_to_all(pack, ('zl', 'c'), 0, 0, tiled=True).reshape(4 * shard, -1)  14.5 us
  transfers between devices with their start and end apart: 31, of which 20 were waited for; matrix products, arithmetic and copies ran while one was open for 26% of the time, Pallas kernels for 0%

profile of v1, /device:TPU:1, one launch (start us, length us, event | category | flops | bytes accessed | tf_op | source)
XLA Modules:
  0.0 390.5 jit_solution(6107935189365569579)
XLA Ops:
  13.0 14.5 %all_to_all.25 = bf16[4,18,3584]{2,1,0:T(8,128)(2,1)S(1)} all-to-all(bf16[4,18,3584]{2,1,0:T(8,128)(2,1)S(1)} %fusion.37), channel_id=1, replica_groups=mesh['y'=4,'x'=4,'zl'=2,'c'=2,'t'=2] {'zl','c'}, dimensions={0} | all-to-all | bytes 1032192 | tf_op jit(solution)/shard_map/all_to_all | solution.py:131
  28.7 39.9 %all_to_all.26 = bf16[16,72,896]{2,1,0:T(8,128)(2,1)S(1)} all-to-all(bf16[16,72,896]{2,1,0:T(8,128)(2,1)S(1)} %broadcast_in_dim.14), channel_id=1, replica_groups=mesh['y'=4,'x'=4,'zl'=2,'c'=2,'t'=2] {'y','x'}, dimensions={0} | all-to-all | bytes 4128768 | tf_op jit(solution)/shard_map/all_to_all | solution.py:133
  75.5 2.2 broadcast_select_fusion.2
  84.4 3.3 collective-permute-start.1
  87.7 7.1 %collective-permute-done.1 = bf16[128,1152]{1,0:T(8,128)(2,1)S(1)} collective-permute-done((bf16[128,1152]{1,0:T(8,128)(2,1)S(1)}, bf16[128,1152]{1,0:T(8,128)(2,1)S(1)}, u32[]{:S(2)}, u32[]{:S(2)}) %collective-permute-start.1) | collective-permute-done | bytes 294944 | tf_op jit(solution)/shard_map/ppermute | solution.py:22
  101.0 5.0 %collective-permute-done.4 = bf16[128,1152]{1,0:T(8,128)(2,1)S(1)} collective-permute-done((bf16[128,1152]{1,0:T(8,128)(2,1)S(1)}, bf16[128,1152]{1,0:T(8,128)(2,1)S(1)}, u32[]{:S(2)}, u32[]{:S(2)}) %collective-permute-start.4) | collective-permute-done | bytes 294944 | tf_op jit(solution)/shard_map/ppermute | solution.py:22
  106.1 7.2 %collective-permute-done.2 = bf16[128,1152]{1,0:T(8,128)(2,1)S(1)} collective-permute-done((bf16[128,1152]{1,0:T(8,128)(2,1)S(1)}, bf16[128,1152]{1,0:T(8,128)(2,1)S(1)}, u32[]{:S(2)}, u32[]{:S(2)}) %collective-permute-start.2) | collective-permute-done | bytes 294944 | tf_op jit(solution)/shard_map/ppermute | solution.py:22
  113.4 13.2 %collective-permute-start.5 = (bf16[512,1152]{1,0:T(8,128)(2,1)S(1)}, bf16[512,1152]{1,0:T(8,128)(2,1)S(1)}, u32[]{:S(2)}, u32[]{:S(2)}) collective-permute-start(bf16[512,1152]{1,0:T(8,128)(2,1)S(1)} %pad_maximum_fusion.4), channel_id=1, source_target_pairs={{0,2},{2,0},{1,3},{3,1},{4,6},{6,4},{5,7},{7,5},{8,10},{10,8},{9,1... | collective-permute-start | bytes 3538952 | tf_op jit(solution)/shard_map/ppermute | solution.py:22
  130.1 7.8 %fusion.3 = f32[1024,1792]{1,0:T(8,128)S(1)} fusion(bf16[1024,1152]{1,0:T(8,128)(2,1)} %constant_dynamic-update-slice_fusion, bf16[1152,2688]{1,0:T(8,128)(2,1)} %all-gather.2.cloned.1.call-done), kind=kOutput, calls=%fused_computation.14 | convolution fusion | flops 4227858432 | bytes 13828096 | tf_op jit(solution)/shard_map/dot_general | solution.py:54
  140.9 5.4 %convolution_convert_fusion.2 = bf16[1024,1152]{1,0:T(8,128)(2,1)S(1)} fusion(bf16[1024,896]{1,0:T(8,128)(2,1)S(1)} %multiply_convert_fusion.2, bf16[1152,2688]{1,0:T(8,128)(2,1)} %all-gather.2.cloned.1.call-done), kind=kOutput, calls=%fused_computation.7 | convolution fusion | flops 2115108864 | bytes 6258688 | tf_op jit(solution)/shard_map/dot_general | solution.py:62
  146.8 2.5 collective-permute-done.6
  152.4 7.1 %collective-permute-done.7 = bf16[128,1152]{1,0:T(8,128)(2,1)S(1)} collective-permute-done((bf16[128,1152]{1,0:T(8,128)(2,1)S(1)}, bf16[128,1152]{1,0:T(8,128)(2,1)S(1)}, u32[]{:S(2)}, u32[]{:S(2)}) %collective-permute-start.7) | collective-permute-done | bytes 294944 | tf_op jit(solution)/shard_map/ppermute | solution.py:22
  159.5 7.0 %collective-permute-done.9 = bf16[128,1152]{1,0:T(8,128)(2,1)S(1)} collective-permute-done((bf16[128,1152]{1,0:T(8,128)(2,1)S(1)}, bf16[128,1152]{1,0:T(8,128)(2,1)S(1)}, u32[]{:S(2)}, u32[]{:S(2)}) %collective-permute-start.9) | collective-permute-done | bytes 294944 | tf_op jit(solution)/shard_map/ppermute | solution.py:22
  169.7 2.8 collective-permute-start.11
  172.5 5.4 %collective-permute-done.13 = bf16[128,1152]{1,0:T(8,128)(2,1)S(1)} collective-permute-done((bf16[128,1152]{1,0:T(8,128)(2,1)S(1)}, bf16[128,1152]{1,0:T(8,128)(2,1)S(1)}, u32[]{:S(2)}, u32[]{:S(2)}) %collective-permute-start.13) | collective-permute-done | bytes 294944 | tf_op jit(solution)/shard_map/ppermute | solution.py:22
  178.0 7.2 %collective-permute-done.11 = bf16[128,1152]{1,0:T(8,128)(2,1)S(1)} collective-permute-done((bf16[128,1152]{1,0:T(8,128)(2,1)S(1)}, bf16[128,1152]{1,0:T(8,128)(2,1)S(1)}, u32[]{:S(2)}, u32[]{:S(2)}) %collective-permute-start.11) | collective-permute-done | bytes 294944 | tf_op jit(solution)/shard_map/ppermute | solution.py:22
  191.3 2.5 constant_dynamic-update-slice_fusion.5
  193.8 9.2 %multiply_convert_fusion.1 = (bf16[1024,896]{1,0:T(8,128)(2,1)S(1)}, bf16[1024,896]{1,0:T(8,128)(2,1)S(1)}) fusion(f32[1024,1792]{1,0:T(8,128)} %copy-done, bf16[1024,1152]{1,0:T(8,128)(2,1)} %constant_dynamic-update-slice_fusion.5, bf16[1152,2688]{1,0:T(8,128)(2,1)} %all-gather.2.cloned.1.call-done), kind=kOutput, calls=%fused_computation.10 | convolution fusion | flops 2134114304 | bytes 15433728 | tf_op jit(solution)/shard_map/dot_general | solution.py:54
  203.0 5.2 %convolution_convert_fusion.1 = bf16[1024,1152]{1,0:T(8,128)(2,1)S(1)} fusion(bf16[1152,2688]{1,0:T(8,128)(2,1)S(1)} %bitcast.112, bf16[1024,896]{1,0:T(8,128)(2,1)S(1)} %get-tuple-element.49, bf16[1024,896]{1,0:T(8,128)(2,1)S(1)} %get-tuple-element.48), kind=kOutput, calls=%fused_computation.6 | convolution fusion | flops 4236378112 | bytes 10158080 | tf_op jit(solution)/shard_map/dot_general | solution.py:62
  209.7 4.0 %convolution_convert_fusion.3 = bf16[1152,896]{1,0:T(8,128)(2,1)} fusion(bf16[1024,1152]{1,0:T(8,128)(2,1)S(1)} %copy-done.59, bf16[1024,896]{1,0:T(8,128)(2,1)S(1)} %copy-done.24), kind=kOutput, calls=%fused_computation.16 | convolution fusion | flops 2114961408 | bytes 6258688 | tf_op jit(solution)/shard_map/dot_general | solution.py:58
  213.8 6.2 %convolution_convert_fusion = bf16[1152,1792]{1,0:T(8,128)(2,1)S(1)} fusion(bf16[1024,1152]{1,0:T(8,128)(2,1)} %constant_dynamic-update-slice_fusion, bf16[1024,896]{1,0:T(8,128)(2,1)S(1)} %get-tuple-element.49, bf16[1024,896]{1,0:T(8,128)(2,1)S(1)} %get-tuple-element.48), kind=kOutput, calls=%fused_computation.1 | convolution fusion | flops 4237262848 | bytes 10158080 | tf_op jit(solution)/shard_map/dot_general | solution.py:58
  223.8 4.7 %pad_maximum_fusion = bf16[1152,2688]{1,0:T(8,128)(2,1)} fusion(bf16[1152,896]{1,0:T(8,128)(2,1)} %convolution_convert_fusion.3, bf16[1152,1792]{1,0:T(8,128)(2,1)S(1)} %convolution_convert_fusion), kind=kLoop, calls=%fused_computation.2 | loop fusion | flops 12386304 | bytes 12386304 | tf_op jit(solution)/shard_map/concatenate | solution.py:214
  228.5 3.1 collective-permute-done.16
  231.7 6.4 %collective-permute-done.18 = bf16[128,1152]{1,0:T(8,128)(2,1)} collective-permute-done((bf16[128,1152]{1,0:T(8,128)(2,1)}, bf16[128,1152]{1,0:T(8,128)(2,1)}, u32[]{:S(2)}, u32[]{:S(2)}) %collective-permute-start.18) | collective-permute-done | bytes 294944 | tf_op jit(solution)/shard_map/ppermute | solution.py:22
  239.6 2.2 fusion.91
  242.8 2.7 collective-permute-start.20
  246.9 5.7 %collective-permute-done.20 = bf16[128,1152]{1,0:T(8,128)(2,1)S(1)} collective-permute-done((bf16[128,1152]{1,0:T(8,128)(2,1)S(1)}, bf16[128,1152]{1,0:T(8,128)(2,1)S(1)}, u32[]{:S(2)}, u32[]{:S(2)}) %collective-permute-start.20) | collective-permute-done | bytes 294944 | tf_op jit(solution)/shard_map/ppermute | solution.py:22
  256.4 2.3 collective-permute-start.24
  258.7 2.3 fusion.29
  266.5 2.2 collective-permute-start.21
  281.4 1.9 subtract_convert_fusion.2
  283.3 2.3 convolution_convert_fusion.6
  292.0 3.5 fusion.25
  295.6 4.7 %broadcast_select_fusion = bf16[1152,896]{0,1:T(8,128)(2,1)S(1)} fusion(pred[]{:T(512)S(6)} %eq.5, bf16[1152,512]{0,1:T(8,128)(2,1)S(1)} %convolution_convert_fusion.5, bf16[1152,256]{0,1:T(8,128)(2,1)S(1)} %copy-done.18, bf16[896]{0:T(1024)(128)(2,1)S(1)} %copy-done.63, bf16[1152,5]{0,1:T(8,128)(2,1)S(1)} %maximum_bitcast_fusion.5, ...), kind=kLoop, calls=%fused_computation.31 | loop fusion | flops 13418496 | bytes 5616641 | tf_op jit(solution)/shard_map/jit(_where)/select_n | solution.py:276
  300.3 3.7 collective-permute-start.25
  304.0 3.7 collective-permute-done.25
  307.8 5.6 %add_convert_fusion = bf16[1152,896]{0,1:T(8,128)(2,1)S(1)} fusion(bf16[1152,896]{0,1:T(8,128)(2,1)S(1)} %collective-permute-done.25, pred[]{:T(512)S(6)} %eq.5, bf16[1152,512]{0,1:T(8,128)(2,1)} %copy-done.12, bf16[1152,256]{0,1:T(8,128)(2,1)S(1)} %copy-done.18, bf16[896]{0:T(1024)(128)(2,1)S(1)} %copy-done.63, ...), kind=kLoop, calls=%fused_computation.4 | loop fusion | flops 17547264 | bytes 7681025 | tf_op jit(solution)/shard_map/convert_element_type | solution.py:277
  313.4 2.5 copy.115
  315.8 3.8 all-to-all-start.2
  319.8 3.1 collective-permute-start.19
  323.0 6.5 %collective-permute-done.10 = bf16[128,1152]{1,0:T(8,128)(2,1)S(1)} collective-permute-done((bf16[128,1152]{1,0:T(8,128)(2,1)S(1)}, bf16[128,1152]{1,0:T(8,128)(2,1)S(1)}, u32[]{:S(2)}, u32[]{:S(2)}) %collective-permute-start.10) | collective-permute-done | bytes 294944 | tf_op jit(solution)/shard_map/ppermute | solution.py:22
  330.5 5.4 %collective-permute-done.19 = bf16[128,1152]{1,0:T(8,128)(2,1)S(1)} collective-permute-done((bf16[128,1152]{1,0:T(8,128)(2,1)S(1)}, bf16[128,1152]{1,0:T(8,128)(2,1)S(1)}, u32[]{:S(2)}, u32[]{:S(2)}) %collective-permute-start.19) | collective-permute-done | bytes 294944 | tf_op jit(solution)/shard_map/ppermute | solution.py:22
  337.2 15.1 %all-to-all-done.2 = bf16[16,72,896]{2,1,0:T(8,128)(2,1)S(1)} async-done(((bf16[16,72,896]{2,1,0:T(8,128)(2,1)}), bf16[16,72,896]{2,1,0:T(8,128)(2,1)S(1)}, u32[]{:S(2)}, u32[]{:S(2)}) %all-to-all-start.2) | async-done | bytes 2064416 | tf_op jit(solution)/shard_map/all_to_all | solution.py:278
  354.8 4.5 %all-to-all-start.3 = ((bf16[4,18,896]{2,1,0:T(8,128)(2,1)}), bf16[4,18,896]{2,1,0:T(8,128)(2,1)S(1)}, u32[]{:S(2)}, u32[]{:S(2)}) async-start(bf16[4,18,896]{2,1,0:T(8,128)(2,1)} %reshape.204), calls=%async_computation.3 | async-start | bytes 344064 | tf_op jit(solution)/shard_map/all_to_all | solution.py:280
  359.4 2.8 fusion.22
  365.9 1.9 reshape.205
  367.9 4.6 %all-to-all-start.4 = ((bf16[4,18,2688]{2,1,0:T(8,128)(2,1)}), bf16[4,18,2688]{2,1,0:T(8,128)(2,1)S(1)}, u32[]{:S(2)}, u32[]{:S(2)}) async-start(bf16[4,18,2688]{2,1,0:T(8,128)(2,1)} %reshape.205), calls=%async_computation.4 | async-start | bytes 1032192 | tf_op jit(solution)/shard_map/all_to_all | solution.py:218
  373.8 6.5 %all-to-all-done.4 = bf16[4,18,2688]{2,1,0:T(8,128)(2,1)S(1)} async-done(((bf16[4,18,2688]{2,1,0:T(8,128)(2,1)}), bf16[4,18,2688]{2,1,0:T(8,128)(2,1)S(1)}, u32[]{:S(2)}, u32[]{:S(2)}) %all-to-all-start.4) | async-done | bytes 387104 | tf_op jit(solution)/shard_map/all_to_all | solution.py:218
  (346 shorter events, 96.4 us)
Async XLA Ops:
  7.2 123.0 %all-gather.2.cloned.1.call-start = ((), (), s32[]{:S(2)}) async-start(), calls=%async_computation.6 | async-start | bytes 6580224 | tf_op jit(solution)/shard_map/all_gather | solution.py:136
  28.5 337.5 %reduce-scatter.4.cloned.1.call-start = ((), (), s32[]{:S(2)}) async-start(), calls=%async_computation.7 | async-start | bytes 6580224
  69.9 5.6 %collective-permute-start = (bf16[1152,768]{1,0:T(8,128)(2,1)}, bf16[1152,768]{1,0:T(8,128)(2,1)}, u32[]{:S(2)}, u32[]{:S(2)}) collective-permute-start(bf16[1152,768]{1,0:T(8,128)(2,1)} %slice.278), channel_id=1, source_target_pairs={{0,2},{2,0},{1,3},{3,1},{4,6},{6,4},{5,7},{7,5},{8,10},{10,8},{9,1... | collective-permute-start | bytes 5308424 | tf_op jit(solution)/shard_map/ppermute | solution.py:22
  84.4 10.4 %collective-permute-start.1 = (bf16[128,1152]{1,0:T(8,128)(2,1)S(1)}, bf16[128,1152]{1,0:T(8,128)(2,1)S(1)}, u32[]{:S(2)}, u32[]{:S(2)}) collective-permute-start(bf16[128,1152]{1,0:T(8,128)(2,1)S(1)} %dynamic-slice_convert_fusion), channel_id=1, source_target_pairs={{0,1},{1,0},{2,3},{3,2},{4,5},{5,4},{6,7},{7,6},{8,9},{9,8},{10,11... | collective-permute-start | bytes 884744 | tf_op jit(solution)/shard_map/ppermute | solution.py:22
  94.8 18.5 %copy-start.13 = (bf16[128,1152]{1,0:T(8,128)(2,1)}, bf16[128,1152]{1,0:T(8,128)(2,1)S(1)}, u32[]{:S(2)}) copy-start(bf16[128,1152]{1,0:T(8,128)(2,1)S(1)} %collective-permute-done.1) | copy-start | bytes 884740
  95.5 17.9 %copy-start.74 = (f32[128]{0:T(128)}, f32[128]{0:T(128)S(1)}, u32[]{:S(2)}) copy-start(f32[128]{0:T(128)S(1)} %get-tuple-element.98) | copy-start | bytes 1540
  96.3 31.0 %copy-start.76 = (f32[128]{0:T(128)}, f32[128]{0:T(128)S(1)}, u32[]{:S(2)}) copy-start(f32[128]{0:T(128)S(1)} %get-tuple-element.100) | copy-start | bytes 1540
  97.2 8.9 %collective-permute-start.4 = (bf16[128,1152]{1,0:T(8,128)(2,1)S(1)}, bf16[128,1152]{1,0:T(8,128)(2,1)S(1)}, u32[]{:S(2)}, u32[]{:S(2)}) collective-permute-start(bf16[128,1152]{1,0:T(8,128)(2,1)S(1)} %get-tuple-element.45), channel_id=1, source_target_pairs={{0,5},{1,4},{4,1},{5,0},{2,7},{3,6},{6,3},{7,2},{8,13},{9,12},{12,... | collective-permute-start | bytes 884744 | tf_op jit(solution)/shard_map/ppermute | solution.py:22
  98.3 7.8 %collective-permute-start.3 = (bf16[128,1152]{1,0:T(8,128)(2,1)S(1)}, bf16[128,1152]{1,0:T(8,128)(2,1)S(1)}, u32[]{:S(2)}, u32[]{:S(2)}) collective-permute-start(bf16[128,1152]{1,0:T(8,128)(2,1)S(1)} %get-tuple-element.45), channel_id=1, source_target_pairs={{0,4},{1,5},{4,0},{5,1},{2,6},{3,7},{6,2},{7,3},{8,12},{9,13},{12,... | collective-permute-start | bytes 884744 | tf_op jit(solution)/shard_map/ppermute | solution.py:22
  99.6 13.7 %collective-permute-start.2 = (bf16[128,1152]{1,0:T(8,128)(2,1)S(1)}, bf16[128,1152]{1,0:T(8,128)(2,1)S(1)}, u32[]{:S(2)}, u32[]{:S(2)}) collective-permute-start(bf16[128,1152]{1,0:T(8,128)(2,1)S(1)} %get-tuple-element.45), channel_id=1, source_target_pairs={{0,1},{1,0},{4,5},{5,4},{2,3},{3,2},{6,7},{7,6},{8,9},{9,8},{12,13... | collective-permute-start | bytes 884744 | tf_op jit(solution)/shard_map/ppermute | solution.py:22
  113.4 15.6 %collective-permute-start.5 = (bf16[512,1152]{1,0:T(8,128)(2,1)S(1)}, bf16[512,1152]{1,0:T(8,128)(2,1)S(1)}, u32[]{:S(2)}, u32[]{:S(2)}) collective-permute-start(bf16[512,1152]{1,0:T(8,128)(2,1)S(1)} %pad_maximum_fusion.4), channel_id=1, source_target_pairs={{0,2},{2,0},{1,3},{3,1},{4,6},{6,4},{5,7},{7,5},{8,10},{10,8},{9,1... | collective-permute-start | bytes 3538952 | tf_op jit(solution)/shard_map/ppermute | solution.py:22
  146.3 2.9 collective-permute-start.6
  149.5 17.2 %copy-start.9 = (bf16[256,1152]{1,0:T(8,128)(2,1)S(1)}, bf16[256,1152]{1,0:T(8,128)(2,1)}, u32[]{:S(2)}) copy-start(bf16[256,1152]{1,0:T(8,128)(2,1)} %param.18) | copy-start | bytes 1769476
  149.6 17.2 %copy-start.56 = (f32[1152]{0:T(1024)S(1)}, f32[1152]{0:T(1024)}, u32[]{:S(2)}) copy-start(f32[1152]{0:T(1024)} %get-tuple-element.27) | copy-start | bytes 13828
  149.6 9.8 %collective-permute-start.7 = (bf16[128,1152]{1,0:T(8,128)(2,1)S(1)}, bf16[128,1152]{1,0:T(8,128)(2,1)S(1)}, u32[]{:S(2)}, u32[]{:S(2)}) collective-permute-start(bf16[128,1152]{1,0:T(8,128)(2,1)S(1)} %get-tuple-element.55), channel_id=1, source_target_pairs={{0,1},{1,0},{4,5},{5,4},{2,3},{3,2},{6,7},{7,6},{8,9},{9,8},{12,13... | collective-permute-start | bytes 884744 | tf_op jit(solution)/shard_map/ppermute | solution.py:22
  151.3 15.2 %collective-permute-start.9 = (bf16[128,1152]{1,0:T(8,128)(2,1)S(1)}, bf16[128,1152]{1,0:T(8,128)(2,1)S(1)}, u32[]{:S(2)}, u32[]{:S(2)}) collective-permute-start(bf16[128,1152]{1,0:T(8,128)(2,1)S(1)} %get-tuple-element.56), channel_id=1, source_target_pairs={{0,5},{1,4},{4,1},{5,0},{2,7},{3,6},{6,3},{7,2},{8,13},{9,12},{12,... | collective-permute-start | bytes 884744 | tf_op jit(solution)/shard_map/ppermute | solution.py:22
  151.9 14.6 %collective-permute-start.8 = (bf16[128,1152]{1,0:T(8,128)(2,1)S(1)}, bf16[128,1152]{1,0:T(8,128)(2,1)S(1)}, u32[]{:S(2)}, u32[]{:S(2)}) collective-permute-start(bf16[128,1152]{1,0:T(8,128)(2,1)S(1)} %get-tuple-element.57), channel_id=1, source_target_pairs={{0,4},{1,5},{4,0},{5,1},{2,6},{3,7},{6,2},{7,3},{8,12},{9,13},{12,... | collective-permute-start | bytes 884744 | tf_op jit(solution)/shard_map/ppermute | solution.py:22
  168.7 9.3 %collective-permute-start.13 = (bf16[128,1152]{1,0:T(8,128)(2,1)S(1)}, bf16[128,1152]{1,0:T(8,128)(2,1)S(1)}, u32[]{:S(2)}, u32[]{:S(2)}) collective-permute-start(bf16[128,1152]{1,0:T(8,128)(2,1)S(1)} %get-tuple-element.41), channel_id=1, source_target_pairs={{0,5},{1,4},{4,1},{5,0},{2,7},{3,6},{6,3},{7,2},{8,13},{9,12},{12,... | collective-permute-start | bytes 884744 | tf_op jit(solution)/shard_map/ppermute | solution.py:22
  169.7 8.2 %collective-permute-start.12 = (bf16[128,1152]{1,0:T(8,128)(2,1)S(1)}, bf16[128,1152]{1,0:T(8,128)(2,1)S(1)}, u32[]{:S(2)}, u32[]{:S(2)}) collective-permute-start(bf16[128,1152]{1,0:T(8,128)(2,1)S(1)} %get-tuple-element.41), channel_id=1, source_target_pairs={{0,4},{1,5},{4,0},{5,1},{2,6},{3,7},{6,2},{7,3},{8,12},{9,13},{12,... | collective-permute-start | bytes 884744 | tf_op jit(solution)/shard_map/ppermute | solution.py:22
  169.7 15.4 %collective-permute-start.11 = (bf16[128,1152]{1,0:T(8,128)(2,1)S(1)}, bf16[128,1152]{1,0:T(8,128)(2,1)S(1)}, u32[]{:S(2)}, u32[]{:S(2)}) collective-permute-start(bf16[128,1152]{1,0:T(8,128)(2,1)S(1)} %get-tuple-element.41), channel_id=1, source_target_pairs={{0,1},{1,0},{4,5},{5,4},{2,3},{3,2},{6,7},{7,6},{8,9},{9,8},{12,13... | collective-permute-start | bytes 884744 | tf_op jit(solution)/shard_map/ppermute | solution.py:22
  186.2 5.1 %collective-permute-start.14 = (bf16[512,1152]{1,0:T(8,128)(2,1)}, bf16[512,1152]{1,0:T(8,128)(2,1)}, u32[]{:S(2)}, u32[]{:S(2)}) collective-permute-start(bf16[512,1152]{1,0:T(8,128)(2,1)} %pad_maximum_fusion.5), channel_id=1, source_target_pairs={{0,2},{2,0},{1,3},{3,1},{4,6},{6,4},{5,7},{7,5},{8,10},{10,8},{9,1... | collective-permute-start | bytes 3538952 | tf_op jit(solution)/shard_map/ppermute | solution.py:22
  191.3 11.7 %slice-start = ((s8[6193152]{0:T(1024)(128)(4,1)}), s8[4194304]{0:T(1024)(128)(4,1)S(1)}, s32[]{:S(2)}) async-start(s8[6193152]{0:T(1024)(128)(4,1)} %bitcast.111), calls=%async_computation.8 | async-start | bytes 8388608
  208.3 11.6 %collective-permute-start.15 = (bf16[512,1152]{1,0:T(8,128)(2,1)S(1)}, bf16[512,1152]{1,0:T(8,128)(2,1)S(1)}, u32[]{:S(2)}, u32[]{:S(2)}) collective-permute-start(bf16[512,1152]{1,0:T(8,128)(2,1)S(1)} %slice.308), channel_id=1, source_target_pairs={{0,2},{2,0},{1,3},{3,1},{4,6},{6,4},{5,7},{7,5},{8,10},{10,8},{9,1... | collective-permute-start | bytes 3538952 | tf_op jit(solution)/shard_map/ppermute | solution.py:22
  221.1 10.5 %collective-permute-start.16 = (bf16[128,1152]{1,0:T(8,128)(2,1)}, bf16[128,1152]{1,0:T(8,128)(2,1)}, u32[]{:S(2)}, u32[]{:S(2)}) collective-permute-start(bf16[128,1152]{1,0:T(8,128)(2,1)} %get-tuple-element.52), channel_id=1, source_target_pairs={{0,1},{1,0},{4,5},{5,4},{2,3},{3,2},{6,7},{7,6},{8,9},{9,8},{12,13... | collective-permute-start | bytes 884744 | tf_op jit(solution)/shard_map/ppermute | solution.py:22
  221.4 16.7 %collective-permute-start.18 = (bf16[128,1152]{1,0:T(8,128)(2,1)}, bf16[128,1152]{1,0:T(8,128)(2,1)}, u32[]{:S(2)}, u32[]{:S(2)}) collective-permute-start(bf16[128,1152]{1,0:T(8,128)(2,1)} %get-tuple-element.53), channel_id=1, source_target_pairs={{0,5},{1,4},{4,1},{5,0},{2,7},{3,6},{6,3},{7,2},{8,13},{9,12},{12,... | collective-permute-start | bytes 884744 | tf_op jit(solution)/shard_map/ppermute | solution.py:22
  222.9 15.1 %collective-permute-start.17 = (bf16[128,1152]{1,0:T(8,128)(2,1)}, bf16[128,1152]{1,0:T(8,128)(2,1)}, u32[]{:S(2)}, u32[]{:S(2)}) collective-permute-start(bf16[128,1152]{1,0:T(8,128)(2,1)} %get-tuple-element.54), channel_id=1, source_target_pairs={{0,4},{1,5},{4,0},{5,1},{2,6},{3,7},{6,2},{7,3},{8,12},{9,13},{12,... | collective-permute-start | bytes 884744 | tf_op jit(solution)/shard_map/ppermute | solution.py:22
  228.5 13.2 %copy-start.10 = (bf16[256,1152]{1,0:T(8,128)(2,1)S(1)}, bf16[256,1152]{1,0:T(8,128)(2,1)}, u32[]{:S(2)}) copy-start(bf16[256,1152]{1,0:T(8,128)(2,1)} %param.18) | copy-start | bytes 1769476
  228.5 13.2 %copy-start.14 = (bf16[128,1152]{1,0:T(8,128)(2,1)S(1)}, bf16[128,1152]{1,0:T(8,128)(2,1)}, u32[]{:S(2)}) copy-start(bf16[128,1152]{1,0:T(8,128)(2,1)} %copy-done.13) | copy-start | bytes 884740
  228.5 13.2 %copy-start.75 = (f32[128]{0:T(128)S(1)}, f32[128]{0:T(128)}, u32[]{:S(2)}) copy-start(f32[128]{0:T(128)} %copy-done.74) | copy-start | bytes 1540
  242.0 10.7 %copy-start.4 = (bf16[1152,768]{1,0:T(8,128)(2,1)S(1)}, bf16[1152,768]{1,0:T(8,128)(2,1)}, u32[]{:S(2)}) copy-start(bf16[1152,768]{1,0:T(8,128)(2,1)} %copy-done.2) | copy-start | bytes 5308420
  242.1 4.2 %collective-permute-start.23 = (f32[3,1152]{1,0:T(4,128)S(1)}, f32[3,1152]{1,0:T(4,128)S(1)}, u32[]{:S(2)}, u32[]{:S(2)}) collective-permute-start(f32[3,1152]{1,0:T(4,128)S(1)} %pad_maximum_fusion.25), channel_id=1, source_target_pairs={{0,1},{1,0},{2,3},{3,2},{4,5},{5,4},{6,7},{7,6},{8,9},{9,8},{10,11... | collective-permute-start | bytes 41480 | tf_op jit(solution)/shard_map/ppermute | solution.py:22
  242.8 9.8 %collective-permute-start.20 = (bf16[128,1152]{1,0:T(8,128)(2,1)S(1)}, bf16[128,1152]{1,0:T(8,128)(2,1)S(1)}, u32[]{:S(2)}, u32[]{:S(2)}) collective-permute-start(bf16[128,1152]{1,0:T(8,128)(2,1)S(1)} %subtract_convert_fusion), channel_id=1, source_target_pairs={{0,1},{1,0},{2,3},{3,2},{4,5},{5,4},{6,7},{7,6},{8,9},{9,8},{10,11... | collective-permute-start | bytes 884744 | tf_op jit(solution)/shard_map/ppermute | solution.py:22
  256.4 12.3 %collective-permute-start.24 = (f32[256]{0:T(256)}, f32[256]{0:T(256)}, u32[]{:S(2)}, u32[]{:S(2)}) collective-permute-start(f32[256]{0:T(256)} %get-tuple-element.23), channel_id=1, source_target_pairs={{0,1},{1,0},{2,3},{3,2},{4,5},{5,4},{6,7},{7,6},{8,9},{9,8},{10,11... | collective-permute-start | bytes 3080 | tf_op jit(solution)/shard_map/ppermute | solution.py:22
  263.3 9.4 %collective-permute-start.22 = (bf16[256,512]{1,0:T(8,128)(2,1)}, bf16[256,512]{1,0:T(8,128)(2,1)}, u32[]{:S(2)}, u32[]{:S(2)}) collective-permute-start(bf16[256,512]{1,0:T(8,128)(2,1)} %pad_maximum_fusion.15), channel_id=1, source_target_pairs={{0,1},{1,0},{2,3},{3,2},{4,5},{5,4},{6,7},{7,6},{8,9},{9,8},{10,11... | collective-permute-start | bytes 786440 | tf_op jit(solution)/shard_map/ppermute | solution.py:22
  266.4 29.1 %copy-start.12 = (bf16[1152,512]{0,1:T(8,128)(2,1)}, bf16[1152,512]{0,1:T(8,128)(2,1)S(1)}, u32[]{:S(2)}) copy-start(bf16[1152,512]{0,1:T(8,128)(2,1)S(1)} %convolution_convert_fusion.5) | copy-start | bytes 3538948
  266.4 16.9 %copy-start.55 = (f32[1152]{0:T(1024)S(1)}, f32[1152]{0:T(1024)}, u32[]{:S(2)}) copy-start(f32[1152]{0:T(1024)} %copy-done.54) | copy-start | bytes 13828
  266.5 25.5 %collective-permute-start.21 = (bf16[256,1152]{1,0:T(8,128)(2,1)}, bf16[256,1152]{1,0:T(8,128)(2,1)}, u32[]{:S(2)}, u32[]{:S(2)}) collective-permute-start(bf16[256,1152]{1,0:T(8,128)(2,1)} %convolution_convert_fusion.7), channel_id=1, source_target_pairs={{0,1},{1,0},{2,3},{3,2},{4,5},{5,4},{6,7},{7,6},{8,9},{9,8},{10,11... | collective-permute-start | bytes 1769480 | tf_op jit(solution)/shard_map/ppermute | solution.py:22
  300.3 7.5 %collective-permute-start.25 = (bf16[1152,896]{0,1:T(8,128)(2,1)S(1)}, bf16[1152,896]{0,1:T(8,128)(2,1)S(1)}, u32[]{:S(2)}, u32[]{:S(2)}) collective-permute-start(bf16[1152,896]{0,1:T(8,128)(2,1)S(1)} %broadcast_select_fusion), channel_id=1, source_target_pairs={{0,2},{2,0},{1,3},{3,1},{4,6},{6,4},{5,7},{7,5},{8,10},{10,8},{9,1... | collective-permute-start | bytes 6193160 | tf_op jit(solution)/shard_map/ppermute | solution.py:22
  315.8 36.4 %all-to-all-start.2 = ((bf16[16,72,896]{2,1,0:T(8,128)(2,1)}), bf16[16,72,896]{2,1,0:T(8,128)(2,1)S(1)}, u32[]{:S(2)}, u32[]{:S(2)}) async-start(bf16[16,72,896]{2,1,0:T(8,128)(2,1)} %bitcast.102), calls=%async_computation.2 | async-start | bytes 4128768 | tf_op jit(solution)/shard_map/all_to_all | solution.py:278
  319.7 16.1 %copy-start.29 = (bf16[128,1152]{1,0:T(8,128)(2,1)S(1)}, bf16[128,1152]{1,0:T(8,128)(2,1)}, u32[]{:S(2)}) copy-start(bf16[128,1152]{1,0:T(8,128)(2,1)} %get-tuple-element.38) | copy-start | bytes 884740
  319.7 16.9 %copy-start.80 = (f32[256]{0:T(256)S(1)}, f32[256]{0:T(256)}, u32[]{:S(2)}) copy-start(f32[256]{0:T(256)} %get-tuple-element.20) | copy-start | bytes 3076
  319.7 9.8 %collective-permute-start.10 = (bf16[128,1152]{1,0:T(8,128)(2,1)S(1)}, bf16[128,1152]{1,0:T(8,128)(2,1)S(1)}, u32[]{:S(2)}, u32[]{:S(2)}) collective-permute-start(bf16[128,1152]{1,0:T(8,128)(2,1)S(1)} %copy-done.27), channel_id=1, source_target_pairs={{0,1},{1,0},{2,3},{3,2},{4,5},{5,4},{6,7},{7,6},{8,9},{9,8},{10,11... | collective-permute-start | bytes 884744 | tf_op jit(solution)/shard_map/ppermute | solution.py:22
  319.8 16.0 %collective-permute-start.19 = (bf16[128,1152]{1,0:T(8,128)(2,1)S(1)}, bf16[128,1152]{1,0:T(8,128)(2,1)S(1)}, u32[]{:S(2)}, u32[]{:S(2)}) collective-permute-start(bf16[128,1152]{1,0:T(8,128)(2,1)S(1)} %copy-done.28), channel_id=1, source_target_pairs={{0,1},{1,0},{2,3},{3,2},{4,5},{5,4},{6,7},{7,6},{8,9},{9,8},{10,11... | collective-permute-start | bytes 884744 | tf_op jit(solution)/shard_map/ppermute | solution.py:22
  330.5 28.9 %copy-start.11 = (bf16[256,1152]{1,0:T(8,128)(2,1)S(1)}, bf16[256,1152]{1,0:T(8,128)(2,1)}, u32[]{:S(2)}) copy-start(bf16[256,1152]{1,0:T(8,128)(2,1)} %param.18) | copy-start | bytes 1769476
  330.5 28.9 %copy-start.72 = (f32[256]{0:T(256)S(1)}, f32[256]{0:T(256)}, u32[]{:S(2)}) copy-start(f32[256]{0:T(256)} %copy-done.70) | copy-start | bytes 3076
  330.5 28.9 %copy-start.79 = (f32[256]{0:T(256)S(1)}, f32[256]{0:T(256)}, u32[]{:S(2)}) copy-start(f32[256]{0:T(256)} %get-tuple-element.93) | copy-start | bytes 3076
  354.8 8.5 %all-to-all-start.3 = ((bf16[4,18,896]{2,1,0:T(8,128)(2,1)}), bf16[4,18,896]{2,1,0:T(8,128)(2,1)S(1)}, u32[]{:S(2)}, u32[]{:S(2)}) async-start(bf16[4,18,896]{2,1,0:T(8,128)(2,1)} %reshape.204), calls=%async_computation.3 | async-start | bytes 344064 | tf_op jit(solution)/shard_map/all_to_all | solution.py:280
  367.9 12.5 %all-to-all-start.4 = ((bf16[4,18,2688]{2,1,0:T(8,128)(2,1)}), bf16[4,18,2688]{2,1,0:T(8,128)(2,1)S(1)}, u32[]{:S(2)}, u32[]{:S(2)}) async-start(bf16[4,18,2688]{2,1,0:T(8,128)(2,1)} %reshape.205), calls=%async_computation.4 | async-start | bytes 1032192 | tf_op jit(solution)/shard_map/all_to_all | solution.py:218
  (71 other events, 193.9 us)
Sparse Core Ops, SparseCore 0:
  28.6 75.8 all-gather.1
  228.6 77.9 reduce-scatter.3

commit v2 on v1

--- a/solution.py
+++ b/solution.py
@@ -2,6 +2,8 @@
 import jax.numpy as jnp
 import numpy as np
 from jax import lax
+from jax.experimental import pallas as pl
+from jax.experimental.pallas import tpu as pltpu
 from jax.sharding import Mesh, PartitionSpec as P
 
 D = 1152
@@ -83,6 +85,177 @@
     half = HD // 2
     first, second = field[..., :half], field[..., half:]
     return jnp.concatenate([first * cosine - second * sine, second * cosine + first * sine], axis=-1)
+
+
+def head_places():
+    place = np.full((2, D), -1, np.int32)
+    for row in range(D):
+        group, at = divmod(row, 18)
+        if at < 8:
+            place[at // 4, row] = 4 * group + at % 4
+    return jnp.asarray(np.concatenate([place, np.zeros((6, D), np.int32)]))
+
+
+def one_hot(place_row):
+    rows = lax.broadcasted_iota(jnp.int32, (HD, D), 0)
+    return jnp.where(rows == place_row, 1.0, 0.0).astype(BF)
+
+
+def corner():
+    rows = lax.broadcasted_iota(jnp.int32, (8, 128), 0)
+    return jnp.where(rows == lax.broadcasted_iota(jnp.int32, (8, 128), 1), 1.0, 0.0).astype(BF)
+
+
+def attend_kernel(
+    core, tokens, own, theirs, places, cosine, sine,
+    gains, scales, normed_out, qk_out, values_out, rot_out, probs_out, mixed_out, branch_out,
+):
+    all_gains = contract_cols(corner(), own[:, 768:])
+    gains[...] = all_gains
+    head_row = all_gains[4:5].astype(BF)
+    query_scale = contract_cols(head_row, one_hot(places[0:1]))
+    key_scale = contract_cols(head_row, one_hot(places[1:2]))
+    scales[...] = jnp.concatenate([query_scale, key_scale, jnp.zeros((6, HD), F32)], axis=0)
+    rows = tokens[...].astype(F32)
+    normed = (rows * inverse_rms(rows) * all_gains[0:1]).astype(BF)
+    normed_out[...] = normed
+
+    def run(first, second):
+        cos, sin = cosine[...], sine[...]
+        qk = product(normed, first[:, :768])
+        qk_out[...] = qk
+        values = product(normed, second[:, :HD]).astype(BF)
+        values_out[...] = values
+
+        def prepare(field, scale):
+            return rotate(field * inverse_rms(field) * scale, cos, sin).astype(BF)
+
+        k_rot = prepare(qk[:, 2 * HD :], key_scale)
+        rot_out[:, 2 * HD :] = k_rot
+        causal = lax.broadcasted_iota(jnp.int32, (SEQ, SEQ), 1) <= lax.broadcasted_iota(
+            jnp.int32, (SEQ, SEQ), 0
+        )
+        for head in range(2):
+            at = slice(head * HD, (head + 1) * HD)
+            q_rot = prepare(qk[:, at], query_scale)
+            rot_out[:, at] = q_rot
+            scores = jnp.where(causal, contract_cols(q_rot, k_rot) * SCALE, -1e30)
+            expo = jnp.exp(scores - jnp.max(scores, axis=-1, keepdims=True))
+            probs = expo / jnp.sum(expo, axis=-1, keepdims=True)
+            probs_out[head] = probs
+            mixed_out[:, at] = product(probs.astype(BF), values).astype(BF)
+        branch_out[...] = contract_cols(mixed_out[...], second[:, HD:768])
+
+    @pl.when(core[0] == 0)
+    def _():
+        run(own, theirs)
+
+    @pl.when(core[0] != 0)
+    def _():
+        run(theirs, own)
+
+
+def attend_back_kernel(
+    core, grad, own, theirs, cosine, sine, scales, qk, values, rot, probs,
+    kv_out, grad_q_out, normed_out, query_gain_out,
+):
+    def run(first, second):
+        cos, sin = cosine[...], sine[...]
+        query_scale = scales[0:1]
+        grad_mixed = product(grad[...], second[:, HD:768]).astype(BF)
+        k_rot = rot[:, 2 * HD :]
+        low_values = values[...]
+        grad_k = jnp.zeros((SEQ, HD), F32)
+        grad_v = jnp.zeros((SEQ, HD), F32)
+        gain = jnp.zeros((1, HD), F32)
+        for head in range(2):
+            at = slice(head * HD, (head + 1) * HD)
+            weights = probs[head]
+            back = grad_mixed[:, at]
+            grad_probs = contract_cols(back, low_values)
+            center = jnp.sum(weights * grad_probs, axis=-1, keepdims=True)
+            grad_scores = (weights * (grad_probs - center)).astype(BF)
+            grad_k = grad_k + contract_rows(grad_scores, rot[:, at])
+            grad_v = grad_v + contract_rows(weights.astype(BF), back)
+            grad_rot = product(grad_scores, k_rot) * SCALE
+            field = qk[:, at]
+            grad_field, terms = norm_back(
+                rotate(grad_rot, cos, -sin), field, inverse_rms(field), query_scale
+            )
+            gain = gain + jnp.sum(terms, axis=0, keepdims=True)
+            grad_q_out[:, at] = grad_field.astype(BF)
+        kv_out[:, :HD] = (grad_k * SCALE).astype(BF)
+        kv_out[:, HD:] = grad_v.astype(BF)
+        query_gain_out[...] = jnp.broadcast_to(gain, (8, HD))
+        normed_out[...] = contract_cols(grad_q_out[...], first[:, : 2 * HD]).astype(BF)
+
+    @pl.when(core[0] == 0)
+    def _():
+        run(own, theirs)
+
+    @pl.when(core[0] != 0)
+    def _():
+        run(theirs, own)
+
+
+def finish_kernel(
+    core, tokens, cotangent, hidden_add, own, theirs, places, cosine, sine, gains, scales, normed, qk,
+    kv_own, kv_their, part_own, part_their, grad_q, query_gain, half_gains, grad_branch, mixed,
+    input_grad, keep, give,
+):
+    kv = kv_own[...].astype(F32) + kv_their[...].astype(F32)
+    keys = qk[:, 2 * HD :]
+    grad_keys, key_terms = norm_back(
+        rotate(kv[:, :HD], cosine[...], -sine[...]), keys, inverse_rms(keys), scales[1:2]
+    )
+    key_gain = jnp.sum(key_terms, axis=0, keepdims=True)
+    grad_keys = grad_keys.astype(BF)
+    grad_values = kv[:, HD:].astype(BF)
+
+    def run(first, second, side0, side1):
+        grad_normed = (
+            part_own[...].astype(F32)
+            + part_their[...].astype(F32)
+            + contract_cols(grad_keys, first[:, 2 * HD : 768])
+            + contract_cols(grad_values, second[:, :HD])
+        )
+        rows = tokens[...].astype(F32)
+        add, terms = norm_back(grad_normed, rows, inverse_rms(rows), gains[0:1])
+        input_grad[...] = cotangent[...].astype(F32) + hidden_add[...].astype(F32) + add
+        input_gain = jnp.sum(terms, axis=0, keepdims=True)
+        low = jnp.concatenate([query_gain[0:1], key_gain], axis=1).astype(BF)
+        head_row = product(low[:, :HD], one_hot(places[0:1])) + product(low[:, HD:], one_hot(places[1:2]))
+        sums = jnp.concatenate(
+            [input_gain, half_gains[0:3], head_row, jnp.zeros((3, D), F32)], axis=0
+        ).astype(BF)
+        side0[:, 768:] = contract_rows(sums, corner()).astype(BF)
+        side1[:, 768:] = jnp.zeros((D, 128), BF)
+        turned = normed[...]
+        side0[:, : 2 * HD] = contract_rows(turned, grad_q[...]).astype(BF)
+        side0[:, 2 * HD : 768] = contract_rows(turned, grad_keys).astype(BF)
+        side1[:, :HD] = contract_rows(turned, grad_values).astype(BF)
+        side1[:, HD:768] = contract_rows(grad_branch[...], mixed[...]).astype(BF)
+
+    @pl.when(core[0] == 0)
+    def _():
+        run(own, theirs, keep, give)
+
+    @pl.when(core[0] != 0)
+    def _():
+        run(theirs, own, give, keep)
+
+
+def local(kernel, outs, count, flops):
+    shapes = [jax.ShapeDtypeStruct(shape, dtype) for shape, dtype in outs]
+    return pl.pallas_call(
+        kernel,
+        out_shape=shapes,
+        in_specs=[pl.BlockSpec(memory_space=pltpu.SMEM)]
+        + [pl.BlockSpec(memory_space=pltpu.VMEM)] * count,
+        out_specs=[pl.BlockSpec(memory_space=pltpu.VMEM)] * len(outs),
+        compiler_params=pltpu.CompilerParams(vmem_limit_bytes=48 * 2**20),
+        cost_estimate=pl.CostEstimate(flops=flops, bytes_accessed=8 * 2**20, transcendentals=200000),
+    )
 
 
 def quarters(weight):
@@ -135,38 +308,20 @@
     ).reshape(D, PAD)
     feed_weights = lax.all_gather(got[:, PAD:], PLANE, axis=0, tiled=True)
 
-    gain_cols = att_half[:, 768:773].astype(F32).T
-    norm_gain, post_gain, feed_scale, final_gain = (gain_cols[i][None, :] for i in range(4))
-    head_cols = gain_cols[4].reshape(64, shard)
-    query_scale = head_cols[:, :4].reshape(1, HD)
-    key_scale = head_cols[:, 4:8].reshape(1, HD)
-    own_half = att_half[:, :768]
-    their_half = other_core(own_half)
-    first_half = jnp.where(core == 0, own_half, their_half)
-    second_half = jnp.where(core == 0, their_half, own_half)
+    flag = jnp.reshape(core, (1,)).astype(jnp.int32)
+    their_half = other_core(att_half[:, :768])
     cosine, sine = tables()
-
-    rows = tokens.astype(F32)
-    inv_in = inverse_rms(rows)
-    normed = (rows * inv_in * norm_gain).astype(BF)
-    qk = product(normed, first_half)
-    queries = jnp.stack([qk[:, :HD], qk[:, HD : 2 * HD]])
-    keys = qk[:, 2 * HD :]
-    values = product(normed, second_half[:, :HD]).astype(BF)
-    inv_q = inverse_rms(queries)
-    inv_k = inverse_rms(keys)
-    q_rot = rotate(queries * inv_q * query_scale, cosine, sine).astype(BF)
-    k_rot = rotate(keys * inv_k * key_scale, cosine, sine).astype(BF)
-    scores = jnp.einsum("hqd,kd->hqk", q_rot, k_rot, preferred_element_type=F32) * SCALE
-    causal = jnp.arange(SEQ)[None, :] <= jnp.arange(SEQ)[:, None]
-    scores = jnp.where(causal, scores, -1e30)
-    expo = jnp.exp(scores - jnp.max(scores, axis=-1, keepdims=True))
-    probs_f = expo / jnp.sum(expo, axis=-1, keepdims=True)
-    probs = probs_f.astype(BF)
-    mixed_heads = jnp.einsum("hqk,kd->hqd", probs, values, preferred_element_type=F32).astype(BF)
-    mixed = jnp.concatenate([mixed_heads[0], mixed_heads[1]], axis=1)
-    output_t = second_half[:, HD:]
-    branch_part = contract_cols(mixed, output_t)
+    places = head_places()
+    gains, scales, normed, qk, values, rot, probs_f, mixed, branch_part = local(
+        attend_kernel,
+        [
+            ((8, D), F32), ((8, HD), F32), ((SEQ, D), BF), ((SEQ, 768), F32), ((SEQ, HD), BF),
+            ((SEQ, 768), BF), ((2, SEQ, SEQ), F32), ((SEQ, 2 * HD), BF), ((SEQ, D), F32),
+        ],
+        6,
+        1100000000,
+    )(flag, tokens, att_half, their_half, places, cosine, sine)
+    post_gain, feed_scale, final_gain = (gains[i : i + 1] for i in (1, 2, 3))
 
     def my_half(field):
         return lax.dynamic_slice_in_dim(field, member * HALF, HALF, 0)
@@ -215,71 +370,53 @@
         [contract_rows(all_feed, grad_both).astype(BF), contract_rows(all_grad, activ).astype(BF)], axis=1
     )
     ffn_sums = lax.psum_scatter(ffn_grads, PLANE, scatter_dimension=0, tiled=True)
-    ffn_sums = lax.all_to_all(ffn_sums.reshape(4, shard, 3 * PAD), ("zl", "c"), 0, 0, tiled=True).astype(F32)
-    grad_gate_weight = whole_units(ffn_sums[:, :, :PAD])
-    grad_up_weight = whole_units(ffn_sums[:, :, PAD : 2 * PAD])
-    grad_down = whole_units(ffn_sums[:, :, 2 * PAD :]).T
-
     hidden_add, feed_terms = norm_back(feed_back, hidden, inv_h, feed_scale)
     grad_hidden = upstream + hidden_add
     grad_branch, post_terms = norm_back(grad_hidden, branch, inv_b, post_gain)
     grad_branch = whole_rows(grad_branch.astype(BF))
-    add_all = whole_rows(hidden_add.astype(BF)).astype(F32)
-    grad_hidden_all = cotangent.astype(F32) + add_all
+    add_all = whole_rows(hidden_add.astype(BF))
     half_gains = jnp.stack([jnp.sum(terms, axis=0) for terms in (post_terms, feed_terms, final_terms)])
+    half_gains = jnp.pad(half_gains, ((0, 5), (0, 0)))
     half_gains = half_gains + other_member(half_gains)
 
-    grad_output_t = contract_rows(grad_branch, mixed)
-    grad_mixed = product(grad_branch, output_t).astype(BF)
-    gm = jnp.stack([grad_mixed[:, :HD], grad_mixed[:, HD:]])
-    grad_probs = jnp.einsum("hqd,kd->hqk", gm, values, preferred_element_type=F32)
-    center = jnp.sum(probs_f * grad_probs, axis=-1, keepdims=True)
-    grad_scores = (probs_f * (grad_probs - center)).astype(BF)
-    grad_krot = jnp.einsum("hqk,hqd->kd", grad_scores, q_rot, preferred_element_type=F32) * SCALE
-    grad_values = jnp.einsum("hqk,hqd->kd", probs, gm, preferred_element_type=F32)
-    kv_part = jnp.concatenate([grad_krot, grad_values], axis=1).astype(BF)
-    kv = kv_part.astype(F32) + other_member(kv_part).astype(F32)
-
-    grad_qrot = jnp.einsum("hqk,kd->hqd", grad_scores, k_rot, preferred_element_type=F32) * SCALE
-    grad_queries, query_terms = norm_back(rotate(grad_qrot, cosine, -sine), queries, inv_q, query_scale)
-    query_gain_part = jnp.sum(query_terms, axis=(0, 1))
+    kv_part, grad_q, normed_part, query_gain_part = local(
+        attend_back_kernel,
+        [((SEQ, 2 * HD), BF), ((SEQ, 2 * HD), BF), ((SEQ, D), BF), ((8, HD), F32)],
+        10,
+        1100000000,
+    )(flag, grad_branch, att_half, their_half, cosine, sine, scales, qk, values, rot, probs_f)
+    kv_their = other_member(kv_part)
+    normed_their = other_member(normed_part)
     query_gain_sum = query_gain_part + other_member(query_gain_part)
-    grad_queries = grad_queries.astype(BF)
-    grad_q = jnp.concatenate([grad_queries[0], grad_queries[1]], axis=1)
-    normed_part = contract_cols(grad_q, first_half[:, : 2 * HD]).astype(BF)
-    normed_q = normed_part.astype(F32) + other_member(normed_part).astype(F32)
-
-    grad_keys, key_terms = norm_back(rotate(kv[:, :HD], cosine, -sine), keys, inv_k, key_scale)
-    key_gain_sum = jnp.sum(key_terms, axis=0)
-    grad_keys = grad_keys.astype(BF)
-    grad_values_low = kv[:, HD:].astype(BF)
-    grad_normed = (
-        normed_q
-        + contract_cols(grad_keys, first_half[:, 2 * HD :])
-        + contract_cols(grad_values_low, second_half[:, :HD])
-    )
-    input_add, input_terms = norm_back(grad_normed, rows, inv_in, norm_gain)
-    input_grad = grad_hidden_all + input_add
-    input_gain_sum = jnp.sum(input_terms, axis=0)
-
-    grad_qk = contract_rows(normed, jnp.concatenate([grad_q, grad_keys], axis=1)).astype(BF)
-    grad_v = contract_rows(normed, grad_values_low).astype(BF)
-    head_sums = jnp.pad(
-        jnp.concatenate([query_gain_sum.reshape(64, 4), key_gain_sum.reshape(64, 4)], axis=1),
-        ((0, 0), (0, shard - 8)),
-    ).reshape(1, D)
-    gain_sums = jnp.concatenate([input_gain_sum[None], half_gains, head_sums], axis=0).T
-    gain_sums = jnp.pad(gain_sums.astype(BF), ((0, 0), (0, 123)))
-    side0 = jnp.concatenate([grad_qk, gain_sums], axis=1)
-    side1 = jnp.concatenate([grad_v, grad_output_t.astype(BF), jnp.zeros((D, 128), BF)], axis=1)
-    keep = jnp.where(core == 0, side0, side1)
-    give = jnp.where(core == 0, side1, side0)
+    input_grad, keep, give = local(
+        finish_kernel,
+        [((SEQ, D), F32), ((D, PAD), BF), ((D, PAD), BF)],
+        21,
+        1300000000,
+    )(
+        flag, tokens, cotangent, add_all, att_half, their_half, places, cosine, sine, gains, scales, normed, qk,
+        kv_part, kv_their, normed_part, normed_their, grad_q, query_gain_sum, half_gains, grad_branch, mixed,
+    )
     att_sums = (keep.astype(F32) + other_core(give).astype(F32)).astype(BF)
     att_sums = lax.all_to_all(att_sums.reshape(16, 4 * shard, PAD), PLANE, 0, 0, tiled=True)
     att_sums = jnp.sum(att_sums.astype(F32), axis=0).astype(BF)
     att_sums = lax.all_to_all(att_sums.reshape(4, shard, PAD), ("zl", "c"), 0, 0, tiled=True).astype(F32)
     out0 = att_sums[0] + att_sums[2]
     out1 = att_sums[1] + att_sums[3]
+
+    blocks = ffn_sums.reshape(4, shard, 3 * PAD)
+    place = 2 * lax.axis_index("zl") + core
+    pieces = []
+    for mask in range(4):
+        block = lax.dynamic_index_in_dim(blocks, place ^ mask, 0, keepdims=False)
+        pieces.append(block if mask == 0 else swap(block, ("zl", "c"), mask, 4))
+    arrived = jnp.stack(pieces)
+    ffn_sums = jnp.stack(
+        [lax.dynamic_index_in_dim(arrived, place ^ k, 0, keepdims=False) for k in range(4)]
+    ).astype(F32)
+    grad_gate_weight = whole_units(ffn_sums[:, :, :PAD])
+    grad_up_weight = whole_units(ffn_sums[:, :, PAD : 2 * PAD])
+    grad_down = whole_units(ffn_sums[:, :, 2 * PAD :]).T
     return (
         layer_out,
         input_grad,

time: 393 us -> 366 us (0.931); the launches traced: 391 us -> 359 us
  waiting for transfers between devices: 104 us -> 136 us
  other arithmetic: 50.8 us -> 19.9 us
  matrix products: 57.5 us -> 32.8 us
  Pallas kernels: 0 us -> 15.6 us
  starting transfers between devices: 62.5 us -> 48.5 us
  local copies, waits for them, and re-layouts: 46.1 us -> 36.8 us
    ppermute x26 -> x29, waiting for transfers between devices: 80.7 us -> 110 us  [swap(): return lax.ppermute(field, axes, [(i, i ^ mask) for i in range(size)])]
    pallas_call x0 -> x3, Pallas kernels: none -> 15.6 us  [the longest x1 7.55 us: on_device(): local(finish_kernel, [((SEQ, D), F32), ((D, PAD), BF), ((D, PAD), BF)], 2...]
    ppermute x26 -> x29, starting transfers between devices: 49.5 us -> 40.1 us  [swap(): return lax.ppermute(field, axes, [(i, i ^ mask) for i in range(size)])]
    all_to_all x1, waiting for transfers between devices: 15.1 us -> 22.6 us  [on_device(): lax.all_to_all(att_sums.reshape(16, 4 * shard, PAD), PLANE, 0, 0, tiled=T...]
    reshape x6 -> x1, local copies, waits for them, and re-layouts: 8.26 us -> 1.11 us  [on_device(): blocks = ffn_sums.reshape(4, shard, 3 * PAD)]
    select_n x2 -> x0, other arithmetic: 6.94 us -> none  [the longest x1 4.73 us: on_device(): give = jnp.where(core == 0, side1, side0)]
    all_to_all x1 -> x0, waiting for transfers between devices: 6.54 us -> none  [on_device(): lax.all_to_all(ffn_sums.reshape(4, shard, 3 * PAD), ('zl', 'c'), 0, 0, ti...]
    dot_general x6 -> x2, matrix products: 17.5 us -> 11.3 us  [contract_cols(): lax.dot_general(left, right, (((1,), (1,)), ((), ())), preferred_element_...]
  transfers between devices with their start and end apart: 31 -> 33, of which waited for: 20 -> 24; matrix products, arithmetic and copies ran while one was open for 26% -> 9% of each run, Pallas kernels for 0% -> 4%
where the time goes in v2:
time: 366 us; the launch traced here: 359 us
  waiting for transfers between devices  136 us (37%)
  blocking collectives  54.4 us (15%)
  starting transfers between devices  48.5 us (13%)
  local copies, waits for them, and re-layouts  36.8 us (10%)
  matrix products  32.8 us (9%)
  other arithmetic  19.9 us (5%)
  Pallas kernels  15.6 us (4%)
  between operations  14.9 us (4%)
    ppermute x29, waiting for transfers between devices, swap(): return lax.ppermute(field, axes, [(i, i ^ mask) for i in range(size)])  110 us
    ppermute x29, starting transfers between devices, swap(): return lax.ppermute(field, axes, [(i, i ^ mask) for i in range(size)])  40.1 us
    all_to_all x1, blocking collectives, on_device(): lax.all_to_all(jnp.broadcast_to(att_shard[None], (16, *att_shard.shape)),...  39.9 us
    all_to_all x1, waiting for transfers between devices, on_device(): lax.all_to_all(att_sums.reshape(16, 4 * shard, PAD), PLANE, 0, 0, tiled=T...  22.6 us
    unnamed x77, local copies, waits for them, and re-layouts  17.2 us
    all_to_all x1, blocking collectives, on_device(): lax.all_to_all(pack, ('zl', 'c'), 0, 0, tiled=True).reshape(4 * shard, -1)  14.5 us
    dot_general x2, matrix products, product(): return jnp.dot(left, right, preferred_element_type=F32)  12.6 us
    dot_general x2, matrix products, contract_cols(): lax.dot_general(left, right, (((1,), (1,)), ((), ())), preferred_element_...  11.3 us
  transfers between devices with their start and end apart: 33, of which 24 were waited for; matrix products, arithmetic and copies ran while one was open for 9% of the time, Pallas kernels for 4%

profile of v2, /device:TPU:1, one launch (start us, length us, event | category | flops | bytes accessed | tf_op | source)
XLA Modules:
  0.0 358.9 jit_solution(2355712199703105750)
XLA Ops:
  13.0 14.5 %all_to_all.20 = bf16[4,18,3584]{2,1,0:T(8,128)(2,1)S(1)} all-to-all(bf16[4,18,3584]{2,1,0:T(8,128)(2,1)S(1)} %fusion.14), channel_id=1, replica_groups=mesh['y'=4,'x'=4,'zl'=2,'c'=2,'t'=2] {'zl','c'}, dimensions={0} | all-to-all | bytes 1032192 | tf_op jit(solution)/shard_map/all_to_all | solution.py:304
  28.7 39.9 %all_to_all.21 = bf16[16,72,896]{2,1,0:T(8,128)(2,1)S(1)} all-to-all(bf16[16,72,896]{2,1,0:T(8,128)(2,1)S(1)} %broadcast_in_dim.2), channel_id=1, replica_groups=mesh['y'=4,'x'=4,'zl'=2,'c'=2,'t'=2] {'y','x'}, dimensions={0} | all-to-all | bytes 4128768 | tf_op jit(solution)/shard_map/all_to_all | solution.py:306
  71.2 1.9 collective-permute-start
  73.1 3.5 collective-permute-done.theirs
  80.4 4.7 %shard_map.289 = (f32[8,1152]{1,0:T(8,128)S(1)}, f32[8,256]{1,0:T(8,128)S(1)}, bf16[256,1152]{1,0:T(8,128)(2,1)S(1)}, f32[256,768]{1,0:T(8,128)S(1)}, bf16[256,2...) custom-call(s32[1]{0:T(128)} %bitcast.core, ...), custom_call_target="tpu_custom_call" | custom-call | flops 1100000000 | bytes 8388608 | tf_op jit(solution)/shard_map/pallas_call | solution.py:315
  90.3 3.4 collective-permute-start.1
  94.7 6.2 %collective-permute-done.1 = bf16[128,1152]{1,0:T(8,128)(2,1)S(1)} collective-permute-done((bf16[128,1152]{1,0:T(8,128)(2,1)S(1)}, bf16[128,1152]{1,0:T(8,128)(2,1)S(1)}, u32[]{:S(2)}, u32[]{:S(2)}) %collective-permute-start.1) | collective-permute-done | bytes 294944 | tf_op jit(solution)/shard_map/ppermute | solution.py:24
  107.4 5.1 %collective-permute-done.4 = bf16[128,1152]{1,0:T(8,128)(2,1)S(1)} collective-permute-done((bf16[128,1152]{1,0:T(8,128)(2,1)S(1)}, bf16[128,1152]{1,0:T(8,128)(2,1)S(1)}, u32[]{:S(2)}, u32[]{:S(2)}) %collective-permute-start.4) | collective-permute-done | bytes 294944 | tf_op jit(solution)/shard_map/ppermute | solution.py:24
  112.4 7.2 %collective-permute-done.2 = bf16[128,1152]{1,0:T(8,128)(2,1)S(1)} collective-permute-done((bf16[128,1152]{1,0:T(8,128)(2,1)S(1)}, bf16[128,1152]{1,0:T(8,128)(2,1)S(1)}, u32[]{:S(2)}, u32[]{:S(2)}) %collective-permute-start.2) | collective-permute-done | bytes 294944 | tf_op jit(solution)/shard_map/ppermute | solution.py:24
  119.7 2.3 collective-permute-start.5
  125.6 7.8 %fusion.1 = f32[1024,1792]{1,0:T(8,128)S(1)} fusion(bf16[1024,1152]{1,0:T(8,128)(2,1)} %constant_dynamic-update-slice_fusion, bf16[1152,2688]{1,0:T(8,128)(2,1)} %all-gather.2.cloned.1.call-done), kind=kOutput, calls=%fused_computation.11 | convolution fusion | flops 4227858432 | bytes 13828096 | tf_op jit(solution)/shard_map/dot_general | solution.py:56
  136.2 3.1 convolution_convert_fusion.2
  139.8 2.5 collective-permute-done.6
  142.7 1.6 collective-permute-start.7
  145.4 7.1 %collective-permute-done.7 = bf16[128,1152]{1,0:T(8,128)(2,1)S(1)} collective-permute-done((bf16[128,1152]{1,0:T(8,128)(2,1)S(1)}, bf16[128,1152]{1,0:T(8,128)(2,1)S(1)}, u32[]{:S(2)}, u32[]{:S(2)}) %collective-permute-start.7) | collective-permute-done | bytes 294944 | tf_op jit(solution)/shard_map/ppermute | solution.py:24
  152.5 7.0 %collective-permute-done.9 = bf16[128,1152]{1,0:T(8,128)(2,1)S(1)} collective-permute-done((bf16[128,1152]{1,0:T(8,128)(2,1)S(1)}, bf16[128,1152]{1,0:T(8,128)(2,1)S(1)}, u32[]{:S(2)}, u32[]{:S(2)}) %collective-permute-start.9) | collective-permute-done | bytes 294944 | tf_op jit(solution)/shard_map/ppermute | solution.py:24
  163.1 2.4 collective-permute-start.11
  165.5 5.4 %collective-permute-done.13 = bf16[128,1152]{1,0:T(8,128)(2,1)S(1)} collective-permute-done((bf16[128,1152]{1,0:T(8,128)(2,1)S(1)}, bf16[128,1152]{1,0:T(8,128)(2,1)S(1)}, u32[]{:S(2)}, u32[]{:S(2)}) %collective-permute-start.13) | collective-permute-done | bytes 294944 | tf_op jit(solution)/shard_map/ppermute | solution.py:24
  171.0 7.2 %collective-permute-done.11 = bf16[128,1152]{1,0:T(8,128)(2,1)S(1)} collective-permute-done((bf16[128,1152]{1,0:T(8,128)(2,1)S(1)}, bf16[128,1152]{1,0:T(8,128)(2,1)S(1)}, u32[]{:S(2)}, u32[]{:S(2)}) %collective-permute-start.11) | collective-permute-done | bytes 294944 | tf_op jit(solution)/shard_map/ppermute | solution.py:24
  178.2 1.7 collective-permute-start.14
  180.1 2.4 collective-permute-done.14
  182.6 2.7 convolution_convert_fusion.3
  185.3 4.8 %multiply_convert_fusion.1 = (bf16[1024,896]{1,0:T(8,128)(2,1)S(1)}, bf16[1024,896]{1,0:T(8,128)(2,1)S(1)}) fusion(f32[1024,1792]{1,0:T(8,128)S(1)} %fusion.1, bf16[1024,1152]{1,0:T(8,128)(2,1)S(1)} %constant_dynamic-update-slice_fusion.5, bf16[1152,2688]{1,0:T(8,128)(2,1)S(1)} %copy-done.32), kind=kOutput, calls=%fused_computation.7 | convolution fusion | flops 2134114304 | bytes 15433728 | tf_op jit(solution)/shard_map/dot_general | solution.py:56
  191.9 6.2 %convolution_convert_fusion = bf16[1152,1792]{1,0:T(8,128)(2,1)S(1)} fusion(bf16[1024,1152]{1,0:T(8,128)(2,1)} %constant_dynamic-update-slice_fusion, bf16[1024,896]{1,0:T(8,128)(2,1)S(1)} %get-tuple-element.72, bf16[1024,896]{1,0:T(8,128)(2,1)S(1)} %get-tuple-element.71), kind=kOutput, calls=%fused_computation | convolution fusion | flops 4237262848 | bytes 10158080 | tf_op jit(solution)/shard_map/dot_general | solution.py:60
  198.1 3.0 pad_maximum_fusion
  201.2 8.2 %convolution_convert_fusion.1 = bf16[1024,1152]{1,0:T(8,128)(2,1)S(1)} fusion(bf16[1152,2688]{1,0:T(8,128)(2,1)} %all-gather.2.cloned.1.call-done, bf16[1024,896]{1,0:T(8,128)(2,1)} %copy-done.34, bf16[1024,896]{1,0:T(8,128)(2,1)} %copy-done.33), kind=kOutput, calls=%fused_computation.3 | convolution fusion | flops 4236378112 | bytes 10158080 | tf_op jit(solution)/shard_map/dot_general | solution.py:64
  209.9 2.5 collective-permute-done.15
  218.4 6.2 %collective-permute-done.16 = bf16[128,1152]{1,0:T(8,128)(2,1)S(1)} collective-permute-done((bf16[128,1152]{1,0:T(8,128)(2,1)}, bf16[128,1152]{1,0:T(8,128)(2,1)S(1)}, u32[]{:S(2)}, u32[]{:S(2)}) %collective-permute-start.16) | collective-permute-done | bytes 294944 | tf_op jit(solution)/shard_map/ppermute | solution.py:24
  224.7 7.1 %collective-permute-done.18 = bf16[128,1152]{1,0:T(8,128)(2,1)} collective-permute-done((bf16[128,1152]{1,0:T(8,128)(2,1)}, bf16[128,1152]{1,0:T(8,128)(2,1)}, u32[]{:S(2)}, u32[]{:S(2)}) %collective-permute-start.18) | collective-permute-done | bytes 294944 | tf_op jit(solution)/shard_map/ppermute | solution.py:24
  233.3 1.8 multiply_reduce_fusion.1
  236.1 2.5 collective-permute-start.20
  239.5 6.6 %collective-permute-done.20 = bf16[128,1152]{1,0:T(8,128)(2,1)S(1)} collective-permute-done((bf16[128,1152]{1,0:T(8,128)(2,1)S(1)}, bf16[128,1152]{1,0:T(8,128)(2,1)S(1)}, u32[]{:S(2)}, u32[]{:S(2)}) %collective-permute-start.20) | collective-permute-done | bytes 294944 | tf_op jit(solution)/shard_map/ppermute | solution.py:24
  246.3 3.4 shard_map.290
  249.8 2.0 collective-permute-start.23
  252.8 1.9 collective-permute-start.22
  254.8 3.7 %collective-permute-done.21.kv_their = bf16[256,512]{1,0:T(8,128)(2,1)S(1)} collective-permute-done((bf16[256,512]{1,0:T(8,128)(2,1)S(1)}, bf16[256,512]{1,0:T(8,128)(2,1)S(1)}, u32[]{:S(2)}, u32[]{:S(2)}) %collective-permute-start.21) | collective-permute-done | bytes 262176 | tf_op jit(solution)/shard_map/ppermute | solution.py:24
  258.5 12.3 %collective-permute-done.22.part_their = bf16[256,1152]{1,0:T(8,128)(2,1)S(1)} collective-permute-done((bf16[256,1152]{1,0:T(8,128)(2,1)S(1)}, bf16[256,1152]{1,0:T(8,128)(2,1)S(1)}, u32[]{:S(2)}, u32[]{:S(2)}) %collective-permute-start.22) | collective-permute-done | bytes 589856 | tf_op jit(solution)/shard_map/ppermute | solution.py:24
  270.9 7.6 %shard_map.291 = (f32[256,1152]{1,0:T(8,128)}, bf16[1152,896]{1,0:T(8,128)(2,1)}, bf16[1152,896]{1,0:T(8,128)(2,1)}) custom-call(s32[1]{0:T(128)} %bitcast.core, bf16[256,1152]{1,0:T(8,128)(2,1)S(1)} %copy-done.3, bf16[256,1152]{1,0:T(8,128)(2,1)S(1)} %copy-done.2, bf16[256,1152]{1,0:T(8,128)(2,1)S(1)} %pad_maximum_fusion.7.hidden_add, ...), custom_call_target="tpu_custom_call" | custom-call | flops 1300000000 | bytes 8388608 | tf_op jit(solution)/shard_map/pallas_call | solution.py:391
  278.4 3.7 %collective-permute-start.25 = (bf16[1152,896]{1,0:T(8,128)(2,1)}, bf16[1152,896]{1,0:T(8,128)(2,1)S(1)}, u32[]{:S(2)}, u32[]{:S(2)}) collective-permute-start(bf16[1152,896]{1,0:T(8,128)(2,1)} %get-tuple-element.46), channel_id=1, source_target_pairs={{0,2},{2,0},{1,3},{3,1},{4,6},{6,4},{5,7},{7,5},{8,10},{10,8},{9,1... | collective-permute-start | bytes 6193160 | tf_op jit(solution)/shard_map/ppermute | solution.py:24
  282.2 4.0 %collective-permute-done.25 = bf16[1152,896]{1,0:T(8,128)(2,1)S(1)} collective-permute-done((bf16[1152,896]{1,0:T(8,128)(2,1)}, bf16[1152,896]{1,0:T(8,128)(2,1)S(1)}, u32[]{:S(2)}, u32[]{:S(2)}) %collective-permute-start.25) | collective-permute-done | bytes 2064416 | tf_op jit(solution)/shard_map/ppermute | solution.py:24
  286.1 3.5 add_convert_fusion
  289.6 3.8 %all-to-all-start.2 = ((bf16[16,72,896]{2,1,0:T(8,128)(2,1)}), bf16[16,72,896]{2,1,0:T(8,128)(2,1)S(1)}, u32[]{:S(2)}, u32[]{:S(2)}) async-start(bf16[16,72,896]{2,1,0:T(8,128)(2,1)} %bitcast.14), calls=%async_computation.2 | async-start | bytes 4128768 | tf_op jit(solution)/shard_map/all_to_all | solution.py:401
  294.8 8.6 %collective-permute-done.10 = bf16[128,1152]{1,0:T(8,128)(2,1)S(1)} collective-permute-done((bf16[128,1152]{1,0:T(8,128)(2,1)S(1)}, bf16[128,1152]{1,0:T(8,128)(2,1)S(1)}, u32[]{:S(2)}, u32[]{:S(2)}) %collective-permute-start.10) | collective-permute-done | bytes 294944 | tf_op jit(solution)/shard_map/ppermute | solution.py:24
  303.5 22.6 %all-to-all-done.2 = bf16[16,72,896]{2,1,0:T(8,128)(2,1)S(1)} async-done(((bf16[16,72,896]{2,1,0:T(8,128)(2,1)}), bf16[16,72,896]{2,1,0:T(8,128)(2,1)S(1)}, u32[]{:S(2)}, u32[]{:S(2)}) %all-to-all-start.2) | async-done | bytes 2064416 | tf_op jit(solution)/shard_map/all_to_all | solution.py:401
  327.1 4.5 %all-to-all-start.3 = ((bf16[4,18,896]{2,1,0:T(8,128)(2,1)}), bf16[4,18,896]{2,1,0:T(8,128)(2,1)S(1)}, u32[]{:S(2)}, u32[]{:S(2)}) async-start(bf16[4,18,896]{2,1,0:T(8,128)(2,1)} %reshape.130), calls=%async_computation.3 | async-start | bytes 344064 | tf_op jit(solution)/shard_map/all_to_all | solution.py:403
  332.5 3.1 all-to-all-done.3
  343.3 2.4 collective-permute-done.28
  345.7 2.9 collective-permute-done.27
  (187 shorter events, 65.6 us)
Async XLA Ops:
  7.2 118.5 %all-gather.2.cloned.1.call-start = ((), (), s32[]{:S(2)}) async-start(), calls=%async_computation.5 | async-start | bytes 6580224 | tf_op jit(solution)/shard_map/all_gather | solution.py:309
  28.5 310.3 %reduce-scatter.4.cloned.1.call-start = ((), (), s32[]{:S(2)}) async-start(), calls=%async_computation.6 | async-start | bytes 6580224
  68.6 9.3 %copy-start.3 = (bf16[256,1152]{1,0:T(8,128)(2,1)S(1)}, bf16[256,1152]{1,0:T(8,128)(2,1)}, u32[]{:S(2)}) copy-start(bf16[256,1152]{1,0:T(8,128)(2,1)} %tokens.3) | copy-start | bytes 1769476
  71.2 5.4 %collective-permute-start = (bf16[1152,768]{1,0:T(8,128)(2,1)}, bf16[1152,768]{1,0:T(8,128)(2,1)S(1)}, u32[]{:S(2)}, u32[]{:S(2)}) collective-permute-start(bf16[1152,768]{1,0:T(8,128)(2,1)} %slice.163), channel_id=1, source_target_pairs={{0,2},{2,0},{1,3},{3,1},{4,6},{6,4},{5,7},{7,5},{8,10},{10,8},{9,1... | collective-permute-start | bytes 5308424 | tf_op jit(solution)/shard_map/ppermute | solution.py:24
  90.3 10.6 %collective-permute-start.1 = (bf16[128,1152]{1,0:T(8,128)(2,1)S(1)}, bf16[128,1152]{1,0:T(8,128)(2,1)S(1)}, u32[]{:S(2)}, u32[]{:S(2)}) collective-permute-start(bf16[128,1152]{1,0:T(8,128)(2,1)S(1)} %dynamic-slice_convert_fusion), channel_id=1, source_target_pairs={{0,1},{1,0},{2,3},{3,2},{4,5},{5,4},{6,7},{7,6},{8,9},{9,8},{10,11... | collective-permute-start | bytes 884744 | tf_op jit(solution)/shard_map/ppermute | solution.py:24
  103.5 8.9 %collective-permute-start.4 = (bf16[128,1152]{1,0:T(8,128)(2,1)S(1)}, bf16[128,1152]{1,0:T(8,128)(2,1)S(1)}, u32[]{:S(2)}, u32[]{:S(2)}) collective-permute-start(bf16[128,1152]{1,0:T(8,128)(2,1)S(1)} %get-tuple-element.68), channel_id=1, source_target_pairs={{0,5},{1,4},{4,1},{5,0},{2,7},{3,6},{6,3},{7,2},{8,13},{9,12},{12,... | collective-permute-start | bytes 884744 | tf_op jit(solution)/shard_map/ppermute | solution.py:24
  104.9 7.5 %collective-permute-start.3 = (bf16[128,1152]{1,0:T(8,128)(2,1)S(1)}, bf16[128,1152]{1,0:T(8,128)(2,1)S(1)}, u32[]{:S(2)}, u32[]{:S(2)}) collective-permute-start(bf16[128,1152]{1,0:T(8,128)(2,1)S(1)} %get-tuple-element.68), channel_id=1, source_target_pairs={{0,4},{1,5},{4,0},{5,1},{2,6},{3,7},{6,2},{7,3},{8,12},{9,13},{12,... | collective-permute-start | bytes 884744 | tf_op jit(solution)/shard_map/ppermute | solution.py:24
  105.9 13.7 %collective-permute-start.2 = (bf16[128,1152]{1,0:T(8,128)(2,1)S(1)}, bf16[128,1152]{1,0:T(8,128)(2,1)S(1)}, u32[]{:S(2)}, u32[]{:S(2)}) collective-permute-start(bf16[128,1152]{1,0:T(8,128)(2,1)S(1)} %get-tuple-element.68), channel_id=1, source_target_pairs={{0,1},{1,0},{4,5},{5,4},{2,3},{3,2},{6,7},{7,6},{8,9},{9,8},{12,13... | collective-permute-start | bytes 884744 | tf_op jit(solution)/shard_map/ppermute | solution.py:24
  119.7 4.8 %collective-permute-start.5 = (bf16[512,1152]{1,0:T(8,128)(2,1)S(1)}, bf16[512,1152]{1,0:T(8,128)(2,1)S(1)}, u32[]{:S(2)}, u32[]{:S(2)}) collective-permute-start(bf16[512,1152]{1,0:T(8,128)(2,1)S(1)} %pad_maximum_fusion.4), channel_id=1, source_target_pairs={{0,2},{2,0},{1,3},{3,1},{4,6},{6,4},{5,7},{7,5},{8,10},{10,8},{9,1... | collective-permute-start | bytes 3538952 | tf_op jit(solution)/shard_map/ppermute | solution.py:24
  139.4 2.9 collective-permute-start.6
  142.6 17.2 %copy-start.2 = (bf16[256,1152]{1,0:T(8,128)(2,1)S(1)}, bf16[256,1152]{1,0:T(8,128)(2,1)}, u32[]{:S(2)}) copy-start(bf16[256,1152]{1,0:T(8,128)(2,1)} %cotangent.1) | copy-start | bytes 1769476
  142.7 9.9 %collective-permute-start.7 = (bf16[128,1152]{1,0:T(8,128)(2,1)S(1)}, bf16[128,1152]{1,0:T(8,128)(2,1)S(1)}, u32[]{:S(2)}, u32[]{:S(2)}) collective-permute-start(bf16[128,1152]{1,0:T(8,128)(2,1)S(1)} %get-tuple-element.76), channel_id=1, source_target_pairs={{0,1},{1,0},{4,5},{5,4},{2,3},{3,2},{6,7},{7,6},{8,9},{9,8},{12,13... | collective-permute-start | bytes 884744 | tf_op jit(solution)/shard_map/ppermute | solution.py:24
  144.3 15.2 %collective-permute-start.9 = (bf16[128,1152]{1,0:T(8,128)(2,1)S(1)}, bf16[128,1152]{1,0:T(8,128)(2,1)S(1)}, u32[]{:S(2)}, u32[]{:S(2)}) collective-permute-start(bf16[128,1152]{1,0:T(8,128)(2,1)S(1)} %get-tuple-element.77), channel_id=1, source_target_pairs={{0,5},{1,4},{4,1},{5,0},{2,7},{3,6},{6,3},{7,2},{8,13},{9,12},{12,... | collective-permute-start | bytes 884744 | tf_op jit(solution)/shard_map/ppermute | solution.py:24
  145.0 14.5 %collective-permute-start.8 = (bf16[128,1152]{1,0:T(8,128)(2,1)S(1)}, bf16[128,1152]{1,0:T(8,128)(2,1)S(1)}, u32[]{:S(2)}, u32[]{:S(2)}) collective-permute-start(bf16[128,1152]{1,0:T(8,128)(2,1)S(1)} %get-tuple-element.78), channel_id=1, source_target_pairs={{0,4},{1,5},{4,0},{5,1},{2,6},{3,7},{6,2},{7,3},{8,12},{9,13},{12,... | collective-permute-start | bytes 884744 | tf_op jit(solution)/shard_map/ppermute | solution.py:24
  161.6 9.4 %collective-permute-start.13 = (bf16[128,1152]{1,0:T(8,128)(2,1)S(1)}, bf16[128,1152]{1,0:T(8,128)(2,1)S(1)}, u32[]{:S(2)}, u32[]{:S(2)}) collective-permute-start(bf16[128,1152]{1,0:T(8,128)(2,1)S(1)} %get-tuple-element.64), channel_id=1, source_target_pairs={{0,5},{1,4},{4,1},{5,0},{2,7},{3,6},{6,3},{7,2},{8,13},{9,12},{12,... | collective-permute-start | bytes 884744 | tf_op jit(solution)/shard_map/ppermute | solution.py:24
  163.1 7.9 %collective-permute-start.12 = (bf16[128,1152]{1,0:T(8,128)(2,1)S(1)}, bf16[128,1152]{1,0:T(8,128)(2,1)S(1)}, u32[]{:S(2)}, u32[]{:S(2)}) collective-permute-start(bf16[128,1152]{1,0:T(8,128)(2,1)S(1)} %get-tuple-element.64), channel_id=1, source_target_pairs={{0,4},{1,5},{4,0},{5,1},{2,6},{3,7},{6,2},{7,3},{8,12},{9,13},{12,... | collective-permute-start | bytes 884744 | tf_op jit(solution)/shard_map/ppermute | solution.py:24
  163.1 15.1 %collective-permute-start.11 = (bf16[128,1152]{1,0:T(8,128)(2,1)S(1)}, bf16[128,1152]{1,0:T(8,128)(2,1)S(1)}, u32[]{:S(2)}, u32[]{:S(2)}) collective-permute-start(bf16[128,1152]{1,0:T(8,128)(2,1)S(1)} %get-tuple-element.64), channel_id=1, source_target_pairs={{0,1},{1,0},{4,5},{5,4},{2,3},{3,2},{6,7},{7,6},{8,9},{9,8},{12,13... | collective-permute-start | bytes 884744 | tf_op jit(solution)/shard_map/ppermute | solution.py:24
  178.2 4.2 %collective-permute-start.14 = (bf16[512,1152]{1,0:T(8,128)(2,1)S(1)}, bf16[512,1152]{1,0:T(8,128)(2,1)S(1)}, u32[]{:S(2)}, u32[]{:S(2)}) collective-permute-start(bf16[512,1152]{1,0:T(8,128)(2,1)S(1)} %pad_maximum_fusion.5), channel_id=1, source_target_pairs={{0,2},{2,0},{1,3},{3,1},{4,6},{6,4},{5,7},{7,5},{8,10},{10,8},{9,1... | collective-permute-start | bytes 3538952 | tf_op jit(solution)/shard_map/ppermute | solution.py:24
  209.5 2.9 collective-permute-start.15
  214.7 10.0 %collective-permute-start.16 = (bf16[128,1152]{1,0:T(8,128)(2,1)}, bf16[128,1152]{1,0:T(8,128)(2,1)S(1)}, u32[]{:S(2)}, u32[]{:S(2)}) collective-permute-start(bf16[128,1152]{1,0:T(8,128)(2,1)} %get-tuple-element.73), channel_id=1, source_target_pairs={{0,1},{1,0},{4,5},{5,4},{2,3},{3,2},{6,7},{7,6},{8,9},{9,8},{12,13... | collective-permute-start | bytes 884744 | tf_op jit(solution)/shard_map/ppermute | solution.py:24
  215.2 16.5 %collective-permute-start.18 = (bf16[128,1152]{1,0:T(8,128)(2,1)}, bf16[128,1152]{1,0:T(8,128)(2,1)}, u32[]{:S(2)}, u32[]{:S(2)}) collective-permute-start(bf16[128,1152]{1,0:T(8,128)(2,1)} %get-tuple-element.74), channel_id=1, source_target_pairs={{0,5},{1,4},{4,1},{5,0},{2,7},{3,6},{6,3},{7,2},{8,13},{9,12},{12,... | collective-permute-start | bytes 884744 | tf_op jit(solution)/shard_map/ppermute | solution.py:24
  216.5 15.3 %collective-permute-start.17 = (bf16[128,1152]{1,0:T(8,128)(2,1)}, bf16[128,1152]{1,0:T(8,128)(2,1)}, u32[]{:S(2)}, u32[]{:S(2)}) collective-permute-start(bf16[128,1152]{1,0:T(8,128)(2,1)} %get-tuple-element.75), channel_id=1, source_target_pairs={{0,4},{1,5},{4,0},{5,1},{2,6},{3,7},{6,2},{7,3},{8,12},{9,13},{12,... | collective-permute-start | bytes 884744 | tf_op jit(solution)/shard_map/ppermute | solution.py:24
  218.4 17.3 %copy-start.30 = (f32[128]{0:T(128)S(1)}, f32[128]{0:T(128)}, u32[]{:S(2)}) copy-start(f32[128]{0:T(128)} %copy-done.29) | copy-start | bytes 1540
  218.4 17.3 %copy-start.31 = (f32[128]{0:T(128)S(1)}, f32[128]{0:T(128)}, u32[]{:S(2)}) copy-start(f32[128]{0:T(128)} %get-tuple-element.103) | copy-start | bytes 1540
  235.1 4.4 %collective-permute-start.24 = (f32[8,1152]{1,0:T(8,128)S(1)}, f32[8,1152]{1,0:T(8,128)S(1)}, u32[]{:S(2)}, u32[]{:S(2)}) collective-permute-start(f32[8,1152]{1,0:T(8,128)S(1)} %select_maximum_fusion), channel_id=1, source_target_pairs={{0,1},{1,0},{2,3},{3,2},{4,5},{5,4},{6,7},{7,6},{8,9},{9,8},{10,11... | collective-permute-start | bytes 110600 | tf_op jit(solution)/shard_map/ppermute | solution.py:24
  235.7 10.6 %copy-start.1 = (bf16[1152,768]{1,0:T(8,128)(2,1)S(1)}, bf16[1152,768]{1,0:T(8,128)(2,1)}, u32[]{:S(2)}) copy-start(bf16[1152,768]{1,0:T(8,128)(2,1)} %copy-done) | copy-start | bytes 5308420
  235.7 10.6 %copy-start.5 = (f32[256,768]{1,0:T(8,128)S(1)}, f32[256,768]{1,0:T(8,128)}, u32[]{:S(2)}) copy-start(f32[256,768]{1,0:T(8,128)} %copy-done.4) | copy-start | bytes 2359300
  235.7 10.6 %copy-start.7 = (f32[256,128]{1,0:T(8,128)S(1)}, f32[256,128]{1,0:T(8,128)}, u32[]{:S(2)}) copy-start(f32[256,128]{1,0:T(8,128)} %constant.75.clone.sine) | copy-start | bytes 393220
  235.7 10.6 %copy-start.9 = (f32[256,128]{1,0:T(8,128)S(1)}, f32[256,128]{1,0:T(8,128)}, u32[]{:S(2)}) copy-start(f32[256,128]{1,0:T(8,128)} %constant.74.clone.cosine) | copy-start | bytes 393220
  235.7 10.6 %copy-start.13 = (f32[2,256,256]{2,1,0:T(8,128)S(1)}, f32[2,256,256]{2,1,0:T(8,128)}, u32[]{:S(2)}) copy-start(f32[2,256,256]{2,1,0:T(8,128)} %copy-done.12) | copy-start | bytes 1572868
  235.7 10.6 %copy-start.15 = (bf16[256,768]{1,0:T(8,128)(2,1)S(1)}, bf16[256,768]{1,0:T(8,128)(2,1)}, u32[]{:S(2)}) copy-start(bf16[256,768]{1,0:T(8,128)(2,1)} %copy-done.14) | copy-start | bytes 1179652
  235.8 10.6 %copy-start.21 = (bf16[256,256]{1,0:T(8,128)(2,1)S(1)}, bf16[256,256]{1,0:T(8,128)(2,1)}, u32[]{:S(2)}) copy-start(bf16[256,256]{1,0:T(8,128)(2,1)} %copy-done.20) | copy-start | bytes 393220
  236.1 10.0 %collective-permute-start.20 = (bf16[128,1152]{1,0:T(8,128)(2,1)S(1)}, bf16[128,1152]{1,0:T(8,128)(2,1)S(1)}, u32[]{:S(2)}, u32[]{:S(2)}) collective-permute-start(bf16[128,1152]{1,0:T(8,128)(2,1)S(1)} %get-tuple-element.85), channel_id=1, source_target_pairs={{0,1},{1,0},{2,3},{3,2},{4,5},{5,4},{6,7},{7,6},{8,9},{9,8},{10,11... | collective-permute-start | bytes 884744 | tf_op jit(solution)/shard_map/ppermute | solution.py:24
  238.6 16.1 %collective-permute-start.19 = (bf16[128,1152]{1,0:T(8,128)(2,1)S(1)}, bf16[128,1152]{1,0:T(8,128)(2,1)S(1)}, u32[]{:S(2)}, u32[]{:S(2)}) collective-permute-start(bf16[128,1152]{1,0:T(8,128)(2,1)S(1)} %get-tuple-element.86), channel_id=1, source_target_pairs={{0,1},{1,0},{2,3},{3,2},{4,5},{5,4},{6,7},{7,6},{8,9},{9,8},{10,11... | collective-permute-start | bytes 884744 | tf_op jit(solution)/shard_map/ppermute | solution.py:24
  249.7 21.2 %copy-start.11 = (bf16[256,1152]{1,0:T(8,128)(2,1)S(1)}, bf16[256,1152]{1,0:T(8,128)(2,1)}, u32[]{:S(2)}) copy-start(bf16[256,1152]{1,0:T(8,128)(2,1)} %copy-done.10) | copy-start | bytes 1769476
  249.7 21.2 %copy-start.17 = (bf16[256,512]{1,0:T(8,128)(2,1)S(1)}, bf16[256,512]{1,0:T(8,128)(2,1)}, u32[]{:S(2)}) copy-start(bf16[256,512]{1,0:T(8,128)(2,1)} %copy-done.16) | copy-start | bytes 786436
  249.7 21.1 %copy-start.19 = (s32[8,1152]{1,0:T(8,128)S(1)}, s32[8,1152]{1,0:T(8,128)}, u32[]{:S(2)}) copy-start(s32[8,1152]{1,0:T(8,128)} %constant.76.clone.places) | copy-start | bytes 110596
  249.7 21.1 %copy-start.23 = (f32[8,1152]{1,0:T(8,128)S(1)}, f32[8,1152]{1,0:T(8,128)}, u32[]{:S(2)}) copy-start(f32[8,1152]{1,0:T(8,128)} %copy-done.22) | copy-start | bytes 110596
  249.8 5.1 %collective-permute-start.23 = (f32[8,256]{1,0:T(8,128)S(1)}, f32[8,256]{1,0:T(8,128)S(1)}, u32[]{:S(2)}, u32[]{:S(2)}) collective-permute-start(f32[8,256]{1,0:T(8,128)S(1)} %get-tuple-element.42), channel_id=1, source_target_pairs={{0,1},{1,0},{2,3},{3,2},{4,5},{5,4},{6,7},{7,6},{8,9},{9,8},{10,11... | collective-permute-start | bytes 24584 | tf_op jit(solution)/shard_map/ppermute | solution.py:24
  251.7 6.8 %collective-permute-start.21 = (bf16[256,512]{1,0:T(8,128)(2,1)S(1)}, bf16[256,512]{1,0:T(8,128)(2,1)S(1)}, u32[]{:S(2)}, u32[]{:S(2)}) collective-permute-start(bf16[256,512]{1,0:T(8,128)(2,1)S(1)} %get-tuple-element.39.kv_own), channel_id=1, source_target_pairs={{0,1},{1,0},{2,3},{3,2},{4,5},{5,4},{6,7},{7,6},{8,9},{9,8},{10,11... | collective-permute-start | bytes 786440 | tf_op jit(solution)/shard_map/ppermute | solution.py:24
  252.8 18.1 %collective-permute-start.22 = (bf16[256,1152]{1,0:T(8,128)(2,1)S(1)}, bf16[256,1152]{1,0:T(8,128)(2,1)S(1)}, u32[]{:S(2)}, u32[]{:S(2)}) collective-permute-start(bf16[256,1152]{1,0:T(8,128)(2,1)S(1)} %get-tuple-element.40.part_own), channel_id=1, source_target_pairs={{0,1},{1,0},{2,3},{3,2},{4,5},{5,4},{6,7},{7,6},{8,9},{9,8},{10,11... | collective-permute-start | bytes 1769480 | tf_op jit(solution)/shard_map/ppermute | solution.py:24
  278.4 7.7 %collective-permute-start.25 = (bf16[1152,896]{1,0:T(8,128)(2,1)}, bf16[1152,896]{1,0:T(8,128)(2,1)S(1)}, u32[]{:S(2)}, u32[]{:S(2)}) collective-permute-start(bf16[1152,896]{1,0:T(8,128)(2,1)} %get-tuple-element.46), channel_id=1, source_target_pairs={{0,2},{2,0},{1,3},{3,1},{4,6},{6,4},{5,7},{7,5},{8,10},{10,8},{9,1... | collective-permute-start | bytes 6193160 | tf_op jit(solution)/shard_map/ppermute | solution.py:24
  289.6 36.5 %all-to-all-start.2 = ((bf16[16,72,896]{2,1,0:T(8,128)(2,1)}), bf16[16,72,896]{2,1,0:T(8,128)(2,1)S(1)}, u32[]{:S(2)}, u32[]{:S(2)}) async-start(bf16[16,72,896]{2,1,0:T(8,128)(2,1)} %bitcast.14), calls=%async_computation.2 | async-start | bytes 4128768 | tf_op jit(solution)/shard_map/all_to_all | solution.py:401
  293.5 10.0 %collective-permute-start.10 = (bf16[128,1152]{1,0:T(8,128)(2,1)S(1)}, bf16[128,1152]{1,0:T(8,128)(2,1)S(1)}, u32[]{:S(2)}, u32[]{:S(2)}) collective-permute-start(bf16[128,1152]{1,0:T(8,128)(2,1)S(1)} %copy-done.26), channel_id=1, source_target_pairs={{0,1},{1,0},{2,3},{3,2},{4,5},{5,4},{6,7},{7,6},{8,9},{9,8},{10,11... | collective-permute-start | bytes 884744 | tf_op jit(solution)/shard_map/ppermute | solution.py:24
  327.1 8.4 %all-to-all-start.3 = ((bf16[4,18,896]{2,1,0:T(8,128)(2,1)}), bf16[4,18,896]{2,1,0:T(8,128)(2,1)S(1)}, u32[]{:S(2)}, u32[]{:S(2)}) async-start(bf16[4,18,896]{2,1,0:T(8,128)(2,1)} %reshape.130), calls=%async_computation.3 | async-start | bytes 344064 | tf_op jit(solution)/shard_map/all_to_all | solution.py:403
  340.0 5.7 %collective-permute-start.28 = (bf16[18,2688]{1,0:T(8,128)(2,1)S(1)}, bf16[18,2688]{1,0:T(8,128)(2,1)S(1)}, u32[]{:S(2)}, u32[]{:S(2)}) collective-permute-start(bf16[18,2688]{1,0:T(8,128)(2,1)S(1)} %get-tuple-element.96), channel_id=1, source_target_pairs={{0,6},{2,4},{4,2},{6,0},{1,7},{3,5},{5,3},{7,1},{8,14},{10,12},{12... | collective-permute-start | bytes 290312 | tf_op jit(solution)/shard_map/ppermute | solution.py:24
  341.2 7.4 %collective-permute-start.27 = (bf16[18,2688]{1,0:T(8,128)(2,1)S(1)}, bf16[18,2688]{1,0:T(8,128)(2,1)S(1)}, u32[]{:S(2)}, u32[]{:S(2)}) collective-permute-start(bf16[18,2688]{1,0:T(8,128)(2,1)S(1)} %get-tuple-element.97), channel_id=1, source_target_pairs={{0,4},{2,6},{4,0},{6,2},{1,5},{3,7},{5,1},{7,3},{8,12},{10,14},{12... | collective-permute-start | bytes 290312 | tf_op jit(solution)/shard_map/ppermute | solution.py:24
  342.5 6.0 %collective-permute-start.26 = (bf16[18,2688]{1,0:T(8,128)(2,1)S(1)}, bf16[18,2688]{1,0:T(8,128)(2,1)S(1)}, u32[]{:S(2)}, u32[]{:S(2)}) collective-permute-start(bf16[18,2688]{1,0:T(8,128)(2,1)S(1)} %get-tuple-element.98), channel_id=1, source_target_pairs={{0,2},{2,0},{4,6},{6,4},{1,3},{3,1},{5,7},{7,5},{8,10},{10,8},{12,... | collective-permute-start | bytes 290312 | tf_op jit(solution)/shard_map/ppermute | solution.py:24
  (20 other events, 31.1 us)
Sparse Core Ops, SparseCore 0:
  28.6 75.8 all-gather.1
  201.3 77.8 reduce-scatter.3
